TPU v7x, 128 devices: a whole 4x4x4 slice. The times are simulated.
128 devices in a mesh: dp: 8 (over z_lo, x), ctx: 16 (over z_hi, y, core).
Axes of the slice: x: 4, y: 4, z: 4 (z_hi: 2, z_lo: 2; z = z_hi * 2 + z_lo), core: 2. Of those that a mesh axis runs over, the one named last changes fastest.
Arguments:
- queries: bfloat16 [8, 8192, 2048], P('dp', 'ctx'), may hold values from -216 to 216
- key_rows: bfloat16 [8, 8192, 2048], P('dp', 'ctx'), may hold values from -8 to 8
- value_rows: bfloat16 [8, 8192, 2048], P('dp', 'ctx'), may hold values from -6 to 6
- document_ids: int32 [8, 8192], P('dp', 'ctx'), may hold values from 0 to 7, never falling along the last dimension, each value on 1 to 2048 neighbouring positions
- dilation_offsets: int32 [4, 16], replicated, may hold values from 0 to 1023
Outputs:
- attended: bfloat16 [8, 8192, 2048], P('dp', 'ctx')
All inputs are finite; a program needn't handle non-finite values.
Results may differ from a plain program's by a relative error of at most 0.0035.
Values may be sent and summed in bfloat16 or wider, within the bound.
A program may use at most 192 MiB of HBM per device.

v0:
```python
import math

import jax
import jax.numpy as jnp
from jax import lax
from jax.experimental import pallas as pl
from jax.experimental.pallas import tpu as pltpu
from jax.sharding import PartitionSpec as P

MESH = pl.DeviceIdType.MESH
F32, BF16, I32 = jnp.float32, jnp.bfloat16, jnp.int32
HEADS, HALF, ROWS, DIM, CHUNK = 16, 8, 512, 128, 256
SEL, FAR, FAR3 = 240, 112, 48
REGIONS = ((0, 128, 1), (128, 64, 2), (192, 32, 3), (224, 16, 4))
NEG = -1e30
SCALE2 = math.log2(math.e) / math.sqrt(DIM)


def nt(a, b):
    return lax.dot_general(a, b, (((1,), (1,)), ((), ())), preferred_element_type=F32)


def nn(a, b):
    return jnp.dot(a, b, preferred_element_type=F32)


def split3(x):
    first = x.astype(BF16)
    rest = x - first.astype(F32)
    second = rest.astype(BF16)
    third = (rest - second.astype(F32)).astype(BF16)
    return jnp.concatenate([first, second, third], axis=0)


def fold3(x):
    n = x.shape[0] // 3
    return (x[2 * n :] + x[n : 2 * n]) + x[:n]


def iota(shape, dim):
    return lax.broadcasted_iota(I32, shape, dim)


def attend(problems):
    scores = [nt(q, k) if bias is None else bias(nt(q, k)) for q, k, _, bias in problems]
    tops = [jnp.max(s, axis=1, keepdims=True) for s in scores]
    weights = [jnp.exp2((s - top) * SCALE2).astype(BF16) for s, top in zip(scores, tops)]
    sums = [nn(w, jnp.concatenate([v, jnp.ones_like(v)], axis=1)) for w, (_, _, v, _) in zip(weights, problems)]
    return [(x[:, :DIM] / x[:, DIM:], top * SCALE2 + jnp.log2(x[:, DIM:])) for x, top in zip(sums, tops)]


def far_pieces(chip):
    return (
        (chip % 4 == 3, ((0, FAR),)),
        (chip % 4 == 2, ((64, FAR),)),
        (chip == 1, ((0, 64),)),
        (chip == 5, ((0, 64), (96, FAR))),
        (chip == 4, ((96, FAR),)),
    )


def next_pieces(chip):
    return ((chip % 4 < 2, ((0, FAR3),)), ((chip == 2) | (chip == 3), ((32, FAR3),)))


def kernel(
    q_hbm, k_hbm, v_hbm, docs_ref, off_ref,
    loc_out, far_out, lse_out, lsef_out,
    qv, kv, vv,
    cq, ck, cv, sq, sk, sv, q1in, kp, vp, dqs, dks, dps, pbuf,
    ob, oo_in, os1, o0, loc,
    st_own, st1, lse0, ls_own, ls1, lo_in, lse_loc,
    docs_all, ot_q, ot_k, base_m, causal, bias0, al_own, a0,
    load_sem, store_sem, lse_sem, d_send, d_recv, x_send, x_recv,
    q_send, q_recv, k_send, k_recv, v_send, v_recv, o_send, o_recv,
    oo_send, oo_recv, l_send, l_recv,
):
    me = lax.axis_index("ctx")
    dp = lax.axis_index("dp")
    c = me // 2
    j = me % 2

    def device(steps, core):
        return (dp, ((c + steps + 8) % 8) * 2 + core)

    def remote(src, dst, send, recv, to):
        return pltpu.make_async_remote_copy(
            src_ref=src, dst_ref=dst, send_sem=send, recv_sem=recv, device_id=to, device_id_type=MESH
        )

    def loads(u):
        copies = []
        for half in range(2):
            first = HALF * (1 - j) if half == 0 else HALF * j
            span = pl.ds(pl.multiple_of((first + 2 * u) * DIM, DIM), 2 * DIM)
            for i, (src, dst) in enumerate(((q_hbm, qv), (k_hbm, kv), (v_hbm, vv))):
                copies.append(pltpu.make_async_copy(src.at[0, :, span], dst.at[:, span], load_sem.at[u, half, i]))
        return copies

    for u in range(4):
        for copy in loads(u):
            copy.start()

    for first, count, bits in REGIONS:
        base_m[first : first + count] = iota((count, CHUNK), 1) - (iota((count, CHUNK), 0) << bits)

    barrier = pltpu.get_barrier_semaphore()
    greeted = [(0, 1 - j)] + [(g, core) for g in (-1, 1) for core in (0, 1)]
    for g, core in greeted:
        pl.semaphore_signal(barrier, inc=1, device_id=device(g, core), device_id_type=MESH)
    pl.semaphore_wait(barrier, len(greeted))

    docs_sent = [(0, 1 - j, 0)] + [(g, core, slot) for g, slot in ((-1, 2), (1, 4)) for core in (0, 1)]
    docs_copies = [
        remote(docs_ref, docs_all.at[slot + j], d_send.at[i], d_recv.at[slot + j], device(g, core))
        for i, (g, core, slot) in enumerate(docs_sent)
    ]
    for copy in docs_copies:
        copy.start()
    docs_all[j] = docs_ref[...]

    def source(staged, held, t, which):
        return staged.at[t] if which == 0 else held.at[t, pl.ds(2 * j, 2)]

    def core_of(which):
        return 1 - j if which == 0 else j

    def q_copy(t, which, piece, low, high, d):
        return remote(
            source(sq, cq, t, which).at[:, pl.ds(128 + low, high - low)],
            q1in.at[t, pl.ds(2 * d, 2), pl.ds(low, high - low)],
            q_send.at[which, piece, t], q_recv.at[d, piece, t], device(-1, core_of(which)),
        )

    def kv_copies(t, which, low, high, d):
        return [
            remote(
                source(staged, held, t, which).at[:, pl.ds(192 + low, high - low)],
                dst.at[t, pl.ds(2 * d, 2), pl.ds(low, high - low)],
                send.at[which, t], recv.at[d, t], device(1, core_of(which)),
            )
            for staged, held, dst, send, recv in ((sk, ck, kp, k_send, k_recv), (sv, cv, vp, v_send, v_recv))
        ]

    def each_q(t, which, do):
        for present, pieces in far_pieces(c):

            @pl.when(present)
            def _():
                for piece, (low, high) in enumerate(pieces):
                    do(q_copy(t, which, piece, low, high, j))

    def each_kv(t, which, do):
        for present, pieces in next_pieces(c):

            @pl.when(present)
            def _():
                for low, high in pieces:
                    for copy in kv_copies(t, which, low, high, j):
                        do(copy)

    def exchange(t):
        return [
            remote(src.at[t], dst.at[t, pl.ds(2 * j, 2)], x_send.at[i, t], x_recv.at[i, t], device(0, 1 - j))
            for i, (src, dst) in enumerate(((sq, cq), (sk, ck), (sv, cv)))
        ]

    def picker(h):
        parts = []
        for level, (first, count, bits) in enumerate(REGIONS):
            shift = off_ref[level, h] & ((1 << bits) - 1)
            parts.append(jnp.where(base_m[first : first + count] == shift, 1.0, 0.0))
        return jnp.concatenate(parts, axis=0).astype(BF16)

    def columns(ref, h):
        return ref[:, pl.ds(pl.multiple_of(h * DIM, DIM), DIM)]

    def select(pick, ref, h):
        x = columns(ref, h)
        both = nn(pick, jnp.concatenate([x[:CHUNK], x[CHUNK:]], axis=1)).astype(BF16)
        return both[:, :DIM], both[:, DIM:]

    def start(copy):
        copy.start()

    def select_head(t, _):
        @pl.when(t % 2 == 0)
        def _():
            for copy in loads(t // 2):
                copy.wait()

        for which in range(2):
            h = HALF * (1 - j) + t if which == 0 else HALF * j + t
            pick = picker(h)
            if which == 1:
                pbuf[t] = pick
            for ref, mine, theirs in ((qv, cq, sq), (kv, ck, sk), (vv, cv, sv)):
                for b, part in enumerate(select(pick, ref, h)):
                    if which == 0:
                        theirs[t, b] = part
                    else:
                        mine[t, 2 * j + b] = part
            each_q(t, which, start)
            each_kv(t, which, start)
            if which == 0:
                for copy in exchange(t):
                    copy.start()
        return 0

    lax.fori_loop(0, HALF, select_head, 0)

    def clear_pads(t, _):
        for b in range(2):
            oo_in[t, b, SEL:] = jnp.zeros((CHUNK - SEL, DIM), BF16)
            for d in range(2):
                ob[d, t, b, SEL:] = jnp.zeros((CHUNK - SEL, DIM), BF16)
        return 0

    lax.fori_loop(0, HALF, clear_pads, 0)

    causal[...] = jnp.where(iota((CHUNK, CHUNK), 1) <= iota((CHUNK, CHUNK), 0), 0.0, NEG)
    eye = jnp.where(iota((CHUNK, CHUNK), 1) == iota((CHUNK, CHUNK), 0), 1.0, 0.0).astype(BF16)
    for b in range(2):
        same = docs_ref[:, b * CHUNK : (b + 1) * CHUNK] == iota((DIM, CHUNK), 0)
        q_one = nt(eye, jnp.where(same, 1.0, 0.0).astype(BF16)).astype(BF16)
        k_one = nt(eye, jnp.where(same, 0.0, NEG).astype(BF16)).astype(BF16)
        bias0[b] = nt(q_one, k_one) + causal[...]

    for i, slot in enumerate((1 - j, 2, 3, 4, 5)):
        remote(docs_ref, docs_all.at[slot], d_send.at[i], d_recv.at[slot], device(0, 1 - j)).wait_recv()
    for b in range(2):
        span = slice(b * CHUNK, (b + 1) * CHUNK)
        ones = [jnp.where(docs_all[g, :, span] == iota((8, CHUNK), 0), 1.0, 0.0) for g in range(4)]
        ones.append(jnp.zeros((DIM - 32, CHUNK), F32))
        ot_q[b * DIM : (b + 1) * DIM] = jnp.concatenate(ones, axis=0).astype(BF16)
        for i, slot in enumerate((0, 1, 4, 5)):
            same = docs_all[slot, :, span] == (iota((DIM, CHUNK), 0) & 7)
            ot_k[i, b * DIM : (b + 1) * DIM] = jnp.where(same, 0.0, NEG).astype(BF16)

    lane = iota((1, DIM), 1)

    def keep(ref, index, rows, t, value):
        old = ref[index + (rows,)]
        ref[index + (rows,)] = jnp.where(lane == t, value, old)

    def join(piece):
        return jnp.concatenate([piece(d, b) for d in range(2) for b in range(2)], axis=0)

    def with_docs(q, g, level, t):
        first, count, _ = REGIONS[level]

        def piece(d, b):
            mark = jnp.where((lane >> 3) == 2 * g + d, 1.0, 0.0).astype(BF16)
            return dqs[t, first : first + count, b * DIM : (b + 1) * DIM] * mark

        return jnp.concatenate([q, join(piece)], axis=1)

    def own_q(t, level):
        first, count, _ = REGIONS[level]
        return with_docs(join(lambda d, b: cq[t, 2 * d + b, first : first + count]), 0, level, t)

    def guest_q(t, level):
        first, count, _ = REGIONS[level]
        return with_docs(join(lambda d, b: q1in[t, 2 * d + b, first - 128 : first - 128 + count]), 1, level, t)

    def own_kv(t, level):
        first, count, _ = REGIONS[level]
        span = slice(first, first + count)
        k = join(lambda d, b: ck[t, 2 * d + b, span])
        kd = join(lambda d, b: dks[d, t, span, b * DIM : (b + 1) * DIM])
        return jnp.concatenate([k, kd], axis=1), join(lambda d, b: cv[t, 2 * d + b, span])

    def both_kv(t, level):
        first, count, _ = REGIONS[level]
        span = slice(first - 192, first - 192 + count)
        k = join(lambda d, b: kp[t, 2 * d + b, span])
        kd = join(lambda d, b: dps[d, t, span, b * DIM : (b + 1) * DIM])
        v = join(lambda d, b: vp[t, 2 * d + b, span])
        own_k, own_v = own_kv(t, level)
        return (
            jnp.concatenate([own_k, jnp.concatenate([k, kd], axis=1)], axis=0),
            jnp.concatenate([own_v, v], axis=0),
        )

    def put(t, level, result, out, stats, shift):
        o, lse = result
        first, count, _ = REGIONS[level]
        spot = slice(first - shift, first - shift + count)
        for d in range(2):
            for b in range(2):
                rows = slice((2 * d + b) * count, (2 * d + b + 1) * count)
                out[d, t, b, spot] = o[rows].astype(BF16)
                keep(stats, (d, b), spot, t, lse[rows])

    def near(n):
        return lambda s: s + causal[:n, :n]

    def near_half(n):
        def bias(s):
            return jnp.concatenate([s[:, :n] + causal[:n, :n], s[:, n:]], axis=1)

        return bias

    def partner_out(t):
        return remote(
            ob.at[1 - j, t, :, pl.ds(0, SEL)], oo_in.at[t, :, pl.ds(0, SEL)],
            oo_send.at[t], oo_recv.at[t], device(0, 1 - j),
        )

    def ret_copy(t, piece, low, high, d):
        return remote(
            os1.at[d, t, :, pl.ds(low, high - low)], far_out.at[HALF * j + t, :, pl.ds(low, high - low)],
            o_send.at[d, piece, t], o_recv.at[j, piece, t], device(1, d),
        )

    def own_head(t, _):
        for copy in exchange(t):
            copy.wait_recv()
        pick = pbuf[t]
        dqs[t] = nt(pick, ot_q[...]).astype(BF16)
        for d in range(2):
            dks[d, t] = nt(pick, ot_k[d]).astype(BF16)
            dps[d, t] = nt(pick[192:], ot_k[2 + d]).astype(BF16)

        problems = []
        q = own_q(t, 0)
        k, v = own_kv(t, 0)
        problems.append((q[:CHUNK], k[:CHUNK], v[:CHUNK], near(CHUNK)))
        late = lambda s: jnp.concatenate([s[:, :CHUNK], s[:, CHUNK:] + causal[...]], axis=1)
        problems.append((q[CHUNK:], k, v, late))
        for level in (1, 2, 3):
            problems.append((own_q(t, level),) + own_kv(t, level) + (near(4 * REGIONS[level][1]),))
        for h in (2 * t, 2 * t + 1):
            q, k, v = columns(qv, h), columns(kv, h), columns(vv, h)
            for b in range(2):
                span = slice(b * CHUNK, (b + 1) * CHUNK)
                problems.append((q[span], k[span], v[span], lambda s, b=b: s + bias0[b]))
        results = attend(problems)
        first = tuple(jnp.concatenate(pair, axis=0) for pair in zip(results[0], results[1]))
        for level, result in enumerate([first] + results[2:5]):
            put(t, level, result, ob, st_own, 0)
        for i in range(2):
            for b in range(2):
                span = slice(b * CHUNK, (b + 1) * CHUNK)
                o, lse = results[5 + 2 * i + b]
                o0[2 * t + i, span] = o
                keep(lse0, (), span, 2 * t + i, lse)
        return 0

    lax.fori_loop(0, HALF, own_head, 0)

    plans = (
        (c == 0, "2", ""),
        (c == 1, "34", "34"),
        (c == 5, "34", "3"),
        (c % 4 == 2, "234", ""),
        (c == 3, "4", ""),
        (c == 4, "24", ""),
    )

    def guest_head(t, _):
        for present, pieces in next_pieces(c - 1):

            @pl.when(present & (c >= 1))
            def _():
                for low, high in pieces:
                    for d in range(2):
                        for copy in kv_copies(t, 0, low, high, d):
                            copy.wait_recv()

        for present, pieces in far_pieces(c + 1):

            @pl.when(present & (c <= 6))
            def _():
                for piece, (low, high) in enumerate(pieces):
                    for d in range(2):
                        q_copy(t, 0, piece, low, high, d).wait_recv()

        for present, guests, owns in plans:

            @pl.when(present)
            def _():
                problems = []
                for name in guests:
                    level = int(name) - 1
                    kv_pair = own_kv(t, level) if level == 1 else both_kv(t, level)
                    problems.append((guest_q(t, level),) + kv_pair + (None,))
                for name in owns:
                    level = int(name) - 1
                    n = 4 * REGIONS[level][1]
                    problems.append((own_q(t, level),) + both_kv(t, level) + (near_half(n),))
                results = attend(problems)
                for name, result in zip(guests, results):
                    put(t, int(name) - 1, result, os1, st1, 128)
                for name, result in zip(owns, results[len(guests) :]):
                    put(t, int(name) - 1, result, ob, st_own, 0)

        for present, pieces in far_pieces(c + 1):

            @pl.when(present & (c <= 6))
            def _():
                for piece, (low, high) in enumerate(pieces):
                    for d in range(2):
                        ret_copy(t, piece, low, high, d).start()

        partner_out(t).start()
        return 0

    lax.fori_loop(0, HALF, guest_head, 0)

    for d in range(2):
        for b in range(2):
            ls1[d, b] = st1[d, b].T[:HALF]
            ls_own[d, b] = st_own[d, b].T[:HALF]

    def far_stats(d):
        return remote(ls1.at[d], lsef_out.at[j], l_send.at[1 + d], l_recv.at[1 + j], device(1, d))

    @pl.when(c <= 6)
    def _():
        for d in range(2):
            far_stats(d).start()

    l_own = remote(ls_own.at[1 - j], lo_in, l_send.at[0], l_recv.at[0], device(0, 1 - j))
    l_own.start()
    l_own.wait_recv()

    mine = ls_own[j]
    theirs = lo_in[...]
    lower = jnp.where(j == 0, mine, theirs)
    upper = jnp.where(j == 0, theirs, mine)
    wide = iota((1, CHUNK), 1)
    own = jnp.concatenate([lower[0], upper[0], lower[1], upper[1]], axis=0)
    own = jnp.where(wide < SEL, own, NEG)
    tall = iota((CHUNK, CHUNK), 0)
    own3 = split3(own)
    zeroth = lse0[...].T
    parts = [jnp.concatenate([zeroth[:HEADS, :CHUNK], zeroth[:HEADS, CHUNK:]], axis=0)]
    spread, chosen = [], []
    for level, (first, count, bits) in enumerate(REGIONS):
        hit = ((iota((CHUNK, CHUNK), 1) >> bits) == tall - first) & (tall >= first) & (tall < first + count)
        spread.append(jnp.where(hit, 1.0, 0.0).astype(BF16))
        chosen.append(picked(off_ref, level, bits))
        parts.append(jnp.where(chosen[level], fold3(nn(own3, spread[level])), NEG))
    lse = log_sum(parts)
    back = jnp.zeros((2 * HEADS, CHUNK), F32)
    for level in range(4):
        back = back + fold3(nt(split3(jnp.where(chosen[level], lse, 0.0)), spread[level]))
    al_own[...] = jnp.exp2(own - back)
    lse_loc[...] = lse
    lse_copy = pltpu.make_async_copy(lse_loc, lse_out, lse_sem.at[0])
    lse_copy.start()
    for b in range(2):
        span = slice(b * CHUNK, (b + 1) * CHUNK)
        a0[span] = jnp.exp2(lse0[span] - upright(lse, b))

    def loc_copy(h):
        return pltpu.make_async_copy(loc.at[h], loc_out.at[h], store_sem.at[h])

    own_first = jnp.where(wide < 128, 0, jnp.where(wide < 192, 128, jnp.where(wide < 224, 192, 224)))
    own_bits = jnp.where(wide < 128, 1, jnp.where(wide < 192, 2, jnp.where(wide < 224, 3, 4)))
    own_base = tall - ((wide - own_first) << own_bits)

    def local_head(t, _):
        partner_out(t).wait_recv()
        for which in range(2):
            h = HALF * j + t if which == 0 else HALF * (1 - j) + t
            o1, o2, o3, o4 = [off_ref[i, h] & (2 << i) - 1 for i in range(4)]
            shift = jnp.where(wide < 128, o1, jnp.where(wide < 192, o2, jnp.where(wide < 224, o3, o4)))
            hit = own_base == shift
            for b in range(2):
                span = slice(b * CHUNK, (b + 1) * CHUNK)
                weight = jnp.where(hit, al_own[pl.ds(b * HEADS + h, 1), :], 0.0).astype(BF16)
                mixed = nn(weight, ob[j, t, b] if which == 0 else oo_in[t, b])
                scale = jnp.sum(jnp.where(lane == h, a0[span], 0.0), axis=1, keepdims=True)
                loc[h, span] = (mixed + scale * o0[h, span]).astype(BF16)
            loc_copy(h).start()
        return 0

    lax.fori_loop(0, HALF, local_head, 0)

    for copy in docs_copies:
        copy.wait_send()
    l_own.wait_send()
    lse_copy.wait()

    def drain(t, _):
        for which in range(2):
            each_q(t, which, lambda copy: copy.wait_send())
            each_kv(t, which, lambda copy: copy.wait_send())
        for copy in exchange(t):
            copy.wait_send()
        partner_out(t).wait_send()
        loc_copy(2 * t).wait()
        loc_copy(2 * t + 1).wait()
        return 0

    lax.fori_loop(0, HALF, drain, 0)

    def drain_far(t, _):
        for present, pieces in far_pieces(c + 1):

            @pl.when(present & (c <= 6))
            def _():
                for piece, (low, high) in enumerate(pieces):
                    for d in range(2):
                        ret_copy(t, piece, low, high, d).wait_send()

        for present, pieces in far_pieces(c):

            @pl.when(present)
            def _():
                for piece, (low, high) in enumerate(pieces):
                    for i in range(2):
                        remote(
                            os1.at[0, t, :, pl.ds(low, high - low)],
                            far_out.at[HALF * i + t, :, pl.ds(low, high - low)],
                            o_send.at[0, piece, t], o_recv.at[i, piece, t], device(1, 0),
                        ).wait_recv()

        return 0

    lax.fori_loop(0, HALF, drain_far, 0)

    @pl.when(c <= 6)
    def _():
        for d in range(2):
            far_stats(d).wait_send()

    @pl.when(c >= 1)
    def _():
        for i in range(2):
            remote(ls1.at[0], lsef_out.at[i], l_send.at[1], l_recv.at[1 + i], device(1, 0)).wait_recv()


def picked(off_ref, level, bits):
    head = iota((HEADS, CHUNK), 0)
    shifts = jnp.zeros((HEADS, CHUNK), I32)
    for h in range(HEADS):
        shifts = jnp.where(head == h, off_ref[level, h] & ((1 << bits) - 1), shifts)
    pick = (iota((HEADS, CHUNK), 1) & ((1 << bits) - 1)) == shifts
    return jnp.concatenate([pick, pick], axis=0)


def log_sum(parts):
    top = parts[0]
    for part in parts[1:]:
        top = jnp.maximum(top, part)
    total = jnp.exp2(parts[0] - top)
    for part in parts[1:]:
        total = total + jnp.exp2(part - top)
    return top + jnp.log2(total)


def upright(dense, b):
    pad = jnp.zeros((DIM - HEADS, CHUNK), F32)
    return jnp.concatenate([dense[b * HEADS : (b + 1) * HEADS], pad], axis=0).T


GROUP = 4


def join_kernel(loc_ref, far_ref, lse_ref, lsef_ref, off_ref, out_ref, al_far, a_loc):
    c = lax.axis_index("ctx") // 2
    lane = iota((1, DIM), 1)

    def valid(x):
        return ((x < 64) & (c % 2 == 1)) | ((x >= 64) & (x < 96) & (c % 4 >= 2)) | ((x >= 96) & (x < FAR) & (c >= 2))

    @pl.when(pl.program_id(0) == 0)
    def _():
        far = jnp.concatenate([lsef_ref[0, 0], lsef_ref[1, 0], lsef_ref[0, 1], lsef_ref[1, 1]], axis=0)
        far = jnp.where(valid(lane), far, NEG)
        far3 = split3(far)
        tall = iota((DIM, CHUNK), 0) + DIM
        parts, spread, chosen = [lse_ref[...]], [], []
        for level, (first, count, bits) in enumerate(REGIONS):
            if level > 0:
                hit = ((iota((DIM, CHUNK), 1) >> bits) == tall - first) & (tall >= first) & (tall < first + count)
                spread.append(jnp.where(hit, 1.0, 0.0).astype(BF16))
                chosen.append(picked(off_ref, level, bits))
                parts.append(jnp.where(chosen[-1], fold3(nn(far3, spread[-1])), NEG))
        lse = log_sum(parts)
        back = jnp.zeros((2 * HEADS, DIM), F32)
        for pick, wide in zip(chosen, spread):
            back = back + fold3(nt(split3(jnp.where(pick, lse, 0.0)), wide))
        al_far[...] = jnp.exp2(far - back)
        share = jnp.exp2(lse_ref[...] - lse)
        for b in range(2):
            a_loc[b * CHUNK : (b + 1) * CHUNK] = upright(share, b)

    row = lane + DIM
    first = jnp.where(row < 192, 128, jnp.where(row < 224, 192, 224))
    bits = jnp.where(row < 192, 2, jnp.where(row < 224, 3, 4))
    base = iota((CHUNK, DIM), 0) - ((row - first) << bits)
    sent = valid(iota((DIM, DIM), 0))
    for i in range(GROUP):
        h = pl.program_id(0) * GROUP + i
        o2, o3, o4 = [off_ref[level, h] & (2 << level) - 1 for level in (1, 2, 3)]
        hit = base == jnp.where(row < 192, o2, jnp.where(row < 224, o3, o4))
        for b in range(2):
            span = slice(b * CHUNK, (b + 1) * CHUNK)
            weight = jnp.where(hit, al_far[pl.ds(b * HEADS + h, 1), :], 0.0).astype(BF16)
            mixed = nn(weight, jnp.where(sent, far_ref[i, b], jnp.zeros((DIM, DIM), BF16)))
            scale = jnp.sum(jnp.where(lane == h, a_loc[span], 0.0), axis=1, keepdims=True)
            out_ref[0, span, i * DIM : (i + 1) * DIM] = (mixed + scale * loc_ref[i, span].astype(F32)).astype(BF16)


def on_device(queries, key_rows, value_rows, document_ids, dilation_offsets):
    any_space = pl.BlockSpec(memory_space=pl.ANY)
    smem = pl.BlockSpec(memory_space=pltpu.SMEM)
    dma = pltpu.SemaphoreType.DMA

    def vmem(*shape, kind=BF16):
        return pltpu.VMEM(shape, kind)

    local, far, lse, lse_far = pl.pallas_call(
        kernel,
        out_shape=(
            jax.ShapeDtypeStruct((HEADS, ROWS, DIM), BF16),
            jax.ShapeDtypeStruct((HEADS, 2, DIM, DIM), BF16),
            jax.ShapeDtypeStruct((2 * HEADS, CHUNK), F32),
            jax.ShapeDtypeStruct((2, 2, HALF, DIM), F32),
        ),
        in_specs=[any_space, any_space, any_space, pl.BlockSpec(memory_space=pltpu.VMEM), smem],
        out_specs=(any_space,) * 4,
        scratch_shapes=[
            vmem(ROWS, HEADS * DIM), vmem(ROWS, HEADS * DIM), vmem(ROWS, HEADS * DIM),
            vmem(HALF, 4, SEL, DIM), vmem(HALF, 4, SEL, DIM), vmem(HALF, 4, SEL, DIM),
            vmem(HALF, 2, SEL, DIM), vmem(HALF, 2, SEL, DIM), vmem(HALF, 2, SEL, DIM),
            vmem(HALF, 4, FAR, DIM), vmem(HALF, 4, FAR3, DIM), vmem(HALF, 4, FAR3, DIM),
            vmem(HALF, SEL, CHUNK), vmem(2, HALF, SEL, CHUNK), vmem(2, HALF, FAR3, CHUNK), vmem(HALF, SEL, CHUNK),
            vmem(2, HALF, 2, CHUNK, DIM), vmem(HALF, 2, CHUNK, DIM), vmem(2, HALF, 2, FAR, DIM),
            vmem(HEADS, ROWS, DIM, kind=F32), vmem(HEADS, ROWS, DIM),
            vmem(2, 2, CHUNK, DIM, kind=F32), vmem(2, 2, DIM, DIM, kind=F32), vmem(ROWS, DIM, kind=F32),
            vmem(2, 2, HALF, CHUNK, kind=F32), vmem(2, 2, HALF, DIM, kind=F32), vmem(2, HALF, CHUNK, kind=F32),
            vmem(2 * HEADS, CHUNK, kind=F32),
            vmem(6, 1, ROWS, kind=I32), vmem(2 * DIM, CHUNK), vmem(4, 2 * DIM, CHUNK),
            vmem(SEL, CHUNK, kind=I32), vmem(CHUNK, CHUNK, kind=F32), vmem(2, CHUNK, CHUNK, kind=F32),
            vmem(2 * HEADS, CHUNK, kind=F32), vmem(ROWS, DIM, kind=F32),
            dma((4, 2, 3)), dma((HEADS,)), dma((1,)), dma((5,)), dma((6,)), dma((3, HALF)), dma((3, HALF)),
            dma((2, 2, HALF)), dma((2, 2, HALF)), dma((2, HALF)), dma((2, HALF)), dma((2, HALF)), dma((2, HALF)),
            dma((2, 2, HALF)), dma((2, 2, HALF)), dma((HALF,)), dma((HALF,)), dma((3,)), dma((3,)),
        ],
        compiler_params=pltpu.CompilerParams(collective_id=0, has_side_effects=True, vmem_limit_bytes=56 << 20),
        name="dilated_attention",
    )(queries, key_rows, value_rows, document_ids, dilation_offsets)
    return pl.pallas_call(
        join_kernel,
        grid=(HEADS // GROUP,),
        out_shape=jax.ShapeDtypeStruct((1, ROWS, HEADS * DIM), BF16),
        in_specs=[
            pl.BlockSpec((GROUP, ROWS, DIM), lambda i: (i, 0, 0)),
            pl.BlockSpec((GROUP, 2, DIM, DIM), lambda i: (i, 0, 0, 0)),
            pl.BlockSpec(memory_space=pltpu.VMEM),
            pl.BlockSpec(memory_space=pltpu.VMEM),
            smem,
        ],
        out_specs=pl.BlockSpec((1, ROWS, GROUP * DIM), lambda i: (0, 0, i)),
        scratch_shapes=[vmem(2 * HEADS, DIM, kind=F32), vmem(ROWS, DIM, kind=F32)],
        compiler_params=pltpu.CompilerParams(vmem_limit_bytes=60 << 20),
        name="join_far",
    )(local, far, lse, lse_far, dilation_offsets)


def solution(mesh):
    placed = (P("dp", "ctx", None), P("dp", "ctx", None), P("dp", "ctx", None), P("dp", "ctx"), P())
    return jax.shard_map(
        on_device, mesh=mesh, in_specs=placed, out_specs=P("dp", "ctx", None), check_vma=False
    )
```

profile of v0, /device:TPU:25, one launch (start us, length us, event | category | flops | bytes accessed | tf_op | source)
XLA Modules:
  0.0 51.3 jit_solution(14465990941174992467)
XLA Ops:
  0.0 46.1 %dilated_attention.1 = (bf16[16,512,128]{2,1,0:T(8,128)(2,1)}, bf16[16,2,128,128]{3,2,1,0:T(8,128)(2,1)}, f32[32,256]{1,0:T(8,128)}, f32[2,2,8,128]{3,2,1,0:T(8,128)}) custom-call(bf16[1,512,2048]{2,1,0:T(8,128)(2,1)} %q_hbm.1, bf16[1,512,2048]{2,1,0:T(8,128)(2,1)} %k_hbm.1, bf16[1,512,2048]{2,1,0:T(8,128)(2,1)} %v_hbm.1, s32[1,512]{1,0:T(1,128)} %docs_ref.1, ...), custom_call_target="tpu_custom_call" | custom-call | tf_op jit(solution)/shard_map/dilated_attention/pallas_call | solution.py:617
  46.1 5.1 %join_far.1 = bf16[1,512,2048]{2,1,0:T(8,128)(2,1)} custom-call(bf16[16,512,128]{2,1,0:T(8,128)(2,1)} %get-tuple-element.9.loc_ref, bf16[16,2,128,128]{3,2,1,0:T(8,128)(2,1)} %get-tuple-element.10.far_ref, f32[32,256]{1,0:T(8,128)} %get-tuple-element.11.lse_ref, f32[2,2,8,128]{3,2,1,0:T(8,128)} %get-tuple-element.12.lsef_ref, s32[4,16]{1,0:T(4,128)} %off_ref.3), custom_call_target="tpu_custom_call" | custom-call | tf_op jit(solution)/shard_map/join_far/pallas_call | solution.py:648
where the time goes:
time: 51.5 us; the launch traced here: 51.3 us
  Pallas kernels  51.3 us (100%)
    pallas_call x1, Pallas kernels, on_device(): pl.pallas_call(kernel, out_shape=(jax.ShapeDtypeStruct((HEADS, ROWS, DIM)...  46.1 us
    pallas_call x1, Pallas kernels, on_device(): pl.pallas_call(join_kernel, grid=(HEADS // GROUP,), out_shape=jax.ShapeDt...  5.12 us

commit v1 on v0

--- a/solution.py
+++ b/solution.py
@@ -60,20 +60,17 @@
 
 
 def next_pieces(chip):
-    return ((chip % 4 < 2, ((0, FAR3),)), ((chip == 2) | (chip == 3), ((32, FAR3),)))
+    return ((chip % 4 < 2, (0, FAR3)), ((chip == 2) | (chip == 3), (32, FAR3)))
 
 
 def kernel(
-    q_hbm, k_hbm, v_hbm, docs_ref, off_ref,
+    q_hbm, k_hbm, v_hbm, docs_hbm, off_hbm,
     loc_out, far_out, lse_out, lsef_out,
-    qv, kv, vv,
-    cq, ck, cv, sq, sk, sv, q1in, kp, vp, dqs, dks, dps, pbuf,
+    docs_ref, off_ref, xv, cx, sx, q1in, kvp, dqs, dks, dps, pbuf,
     ob, oo_in, os1, o0, loc,
     st_own, st1, lse0, ls_own, ls1, lo_in, lse_loc,
     docs_all, ot_q, ot_k, base_m, causal, bias0, al_own, a0,
-    load_sem, store_sem, lse_sem, d_send, d_recv, x_send, x_recv,
-    q_send, q_recv, k_send, k_recv, v_send, v_recv, o_send, o_recv,
-    oo_send, oo_recv, l_send, l_recv,
+    load_sem, once, d_recv, x_recv, q_recv, k_recv, l_recv,
 ):
     me = lax.axis_index("ctx")
     dp = lax.axis_index("dp")
@@ -88,82 +85,105 @@
             src_ref=src, dst_ref=dst, send_sem=send, recv_sem=recv, device_id=to, device_id_type=MESH
         )
 
-    def loads(u):
-        copies = []
+    store_sem, lse_sem, d_send, x_send, q_send, k_send, o_send, o_recv, oo_send, oo_recv, l_send, l_own_send = [
+        once.at[i] for i in range(12)
+    ]
+
+    def load_start(u):
         for half in range(2):
             first = HALF * (1 - j) if half == 0 else HALF * j
             span = pl.ds(pl.multiple_of((first + 2 * u) * DIM, DIM), 2 * DIM)
-            for i, (src, dst) in enumerate(((q_hbm, qv), (k_hbm, kv), (v_hbm, vv))):
-                copies.append(pltpu.make_async_copy(src.at[0, :, span], dst.at[:, span], load_sem.at[u, half, i]))
-        return copies
-
+            for i, src in enumerate((q_hbm, k_hbm, v_hbm)):
+                pltpu.make_async_copy(src.at[0, :, span], xv.at[i, :, span], load_sem.at[u]).start()
+
+    def load_wait(u):
+        part = xv.at[:, :, pl.ds(0, 4 * DIM)]
+        pltpu.make_async_copy(part, part, load_sem.at[u]).wait()
+
+    docs_load = pltpu.make_async_copy(docs_hbm, docs_ref, load_sem.at[4])
+    off_load = pltpu.make_async_copy(off_hbm, off_ref, load_sem.at[5])
+    docs_load.start()
+    off_load.start()
     for u in range(4):
-        for copy in loads(u):
-            copy.start()
+        load_start(u)
 
     for first, count, bits in REGIONS:
         base_m[first : first + count] = iota((count, CHUNK), 1) - (iota((count, CHUNK), 0) << bits)
 
+    near_chips = ((1, c <= 6), (-1, c >= 1))
     barrier = pltpu.get_barrier_semaphore()
-    greeted = [(0, 1 - j)] + [(g, core) for g in (-1, 1) for core in (0, 1)]
-    for g, core in greeted:
-        pl.semaphore_signal(barrier, inc=1, device_id=device(g, core), device_id_type=MESH)
-    pl.semaphore_wait(barrier, len(greeted))
-
-    docs_sent = [(0, 1 - j, 0)] + [(g, core, slot) for g, slot in ((-1, 2), (1, 4)) for core in (0, 1)]
-    docs_copies = [
-        remote(docs_ref, docs_all.at[slot + j], d_send.at[i], d_recv.at[slot + j], device(g, core))
-        for i, (g, core, slot) in enumerate(docs_sent)
-    ]
-    for copy in docs_copies:
-        copy.start()
+    pl.semaphore_signal(barrier, inc=1, device_id=device(0, 1 - j), device_id_type=MESH)
+    for g, present in near_chips:
+
+        @pl.when(present)
+        def _():
+            for core in (0, 1):
+                pl.semaphore_signal(barrier, inc=1, device_id=device(g, core), device_id_type=MESH)
+
+    docs_load.wait()
+    off_load.wait()
+    pl.semaphore_wait(barrier, 1 + jnp.where(c <= 6, 2, 0) + jnp.where(c >= 1, 2, 0))
+
+    def docs_copy(g, core, slot):
+        return remote(docs_ref, docs_all.at[slot], d_send, d_recv.at[slot], device(g, core))
+
+    def each_docs(do):
+        do(docs_copy(0, 1 - j, j))
+        for (g, present), first in zip(near_chips, (4, 2)):
+
+            @pl.when(present)
+            def _():
+                for core in (0, 1):
+                    do(docs_copy(g, core, first + j))
+
+    each_docs(lambda copy: copy.start())
     docs_all[j] = docs_ref[...]
-
-    def source(staged, held, t, which):
-        return staged.at[t] if which == 0 else held.at[t, pl.ds(2 * j, 2)]
 
     def core_of(which):
         return 1 - j if which == 0 else j
 
-    def q_copy(t, which, piece, low, high, d):
+    def q_copy(t, which, low, high):
+        rows = pl.ds(128 + low, high - low)
         return remote(
-            source(sq, cq, t, which).at[:, pl.ds(128 + low, high - low)],
-            q1in.at[t, pl.ds(2 * d, 2), pl.ds(low, high - low)],
-            q_send.at[which, piece, t], q_recv.at[d, piece, t], device(-1, core_of(which)),
+            sx.at[t, 0, :, rows] if which == 0 else cx.at[t, 0, pl.ds(2 * j, 2), rows],
+            q1in.at[t, pl.ds(2 * j, 2), pl.ds(low, high - low)],
+            q_send, q_recv.at[t], device(-1, core_of(which)),
         )
 
-    def kv_copies(t, which, low, high, d):
-        return [
-            remote(
-                source(staged, held, t, which).at[:, pl.ds(192 + low, high - low)],
-                dst.at[t, pl.ds(2 * d, 2), pl.ds(low, high - low)],
-                send.at[which, t], recv.at[d, t], device(1, core_of(which)),
-            )
-            for staged, held, dst, send, recv in ((sk, ck, kp, k_send, k_recv), (sv, cv, vp, v_send, v_recv))
-        ]
-
-    def each_q(t, which, do):
+    def kv_copy(t, which, low, high):
+        rows = pl.ds(192 + low, high - low)
+        return remote(
+            sx.at[t, pl.ds(1, 2), :, rows] if which == 0 else cx.at[t, pl.ds(1, 2), pl.ds(2 * j, 2), rows],
+            kvp.at[t, :, pl.ds(2 * j, 2), pl.ds(low, high - low)],
+            k_send, k_recv.at[t], device(1, core_of(which)),
+        )
+
+    def each_q(t, which):
         for present, pieces in far_pieces(c):
-
-            @pl.when(present)
-            def _():
-                for piece, (low, high) in enumerate(pieces):
-                    do(q_copy(t, which, piece, low, high, j))
-
-    def each_kv(t, which, do):
-        for present, pieces in next_pieces(c):
 
             @pl.when(present)
             def _():
                 for low, high in pieces:
-                    for copy in kv_copies(t, which, low, high, j):
-                        do(copy)
+                    q_copy(t, which, low, high).start()
+
+    def each_kv(t, which):
+        for present, (low, high) in next_pieces(c):
+
+            @pl.when(present)
+            def _():
+                kv_copy(t, which, low, high).start()
 
     def exchange(t):
-        return [
-            remote(src.at[t], dst.at[t, pl.ds(2 * j, 2)], x_send.at[i, t], x_recv.at[i, t], device(0, 1 - j))
-            for i, (src, dst) in enumerate(((sq, cq), (sk, ck), (sv, cv)))
-        ]
+        return remote(sx.at[t], cx.at[t, :, pl.ds(2 * j, 2)], x_send, x_recv.at[t], device(0, 1 - j))
+
+    def size_of(pieces):
+        return sum(high - low for low, high in pieces)
+
+    def got(part, sem):
+        remote(part, part, once.at[0], sem, device(0, 1 - j)).wait_recv()
+
+    def sent(part, sem):
+        remote(part, part, sem, once.at[0], device(0, 1 - j)).wait_send()
 
     def picker(h):
         parts = []
@@ -172,39 +192,34 @@
             parts.append(jnp.where(base_m[first : first + count] == shift, 1.0, 0.0))
         return jnp.concatenate(parts, axis=0).astype(BF16)
 
-    def columns(ref, h):
-        return ref[:, pl.ds(pl.multiple_of(h * DIM, DIM), DIM)]
-
-    def select(pick, ref, h):
-        x = columns(ref, h)
+    def columns(i, h):
+        return xv[i, :, pl.ds(pl.multiple_of(h * DIM, DIM), DIM)]
+
+    def select(pick, i, h):
+        x = columns(i, h)
         both = nn(pick, jnp.concatenate([x[:CHUNK], x[CHUNK:]], axis=1)).astype(BF16)
         return both[:, :DIM], both[:, DIM:]
 
-    def start(copy):
-        copy.start()
-
     def select_head(t, _):
         @pl.when(t % 2 == 0)
         def _():
-            for copy in loads(t // 2):
-                copy.wait()
+            load_wait(t // 2)
 
         for which in range(2):
             h = HALF * (1 - j) + t if which == 0 else HALF * j + t
             pick = picker(h)
             if which == 1:
                 pbuf[t] = pick
-            for ref, mine, theirs in ((qv, cq, sq), (kv, ck, sk), (vv, cv, sv)):
-                for b, part in enumerate(select(pick, ref, h)):
+            for i in range(3):
+                for b, part in enumerate(select(pick, i, h)):
                     if which == 0:
-                        theirs[t, b] = part
+                        sx[t, i, b] = part
                     else:
-                        mine[t, 2 * j + b] = part
-            each_q(t, which, start)
-            each_kv(t, which, start)
+                        cx[t, i, 2 * j + b] = part
+            each_q(t, which)
+            each_kv(t, which)
             if which == 0:
-                for copy in exchange(t):
-                    copy.start()
+                exchange(t).start()
         return 0
 
     lax.fori_loop(0, HALF, select_head, 0)
@@ -226,8 +241,19 @@
         k_one = nt(eye, jnp.where(same, 0.0, NEG).astype(BF16)).astype(BF16)
         bias0[b] = nt(q_one, k_one) + causal[...]
 
-    for i, slot in enumerate((1 - j, 2, 3, 4, 5)):
-        remote(docs_ref, docs_all.at[slot], d_send.at[i], d_recv.at[slot], device(0, 1 - j)).wait_recv()
+    docs_copy(0, 1 - j, 1 - j).wait_recv()
+    for (g, present), first in zip(near_chips, (2, 4)):
+
+        @pl.when(present)
+        def _():
+            for core in (0, 1):
+                docs_copy(g, core, first + core).wait_recv()
+
+        @pl.when(jnp.logical_not(present))
+        def _():
+            for core in (0, 1):
+                docs_all[first + core] = docs_ref[...]
+
     for b in range(2):
         span = slice(b * CHUNK, (b + 1) * CHUNK)
         ones = [jnp.where(docs_all[g, :, span] == iota((8, CHUNK), 0), 1.0, 0.0) for g in range(4)]
@@ -257,7 +283,7 @@
 
     def own_q(t, level):
         first, count, _ = REGIONS[level]
-        return with_docs(join(lambda d, b: cq[t, 2 * d + b, first : first + count]), 0, level, t)
+        return with_docs(join(lambda d, b: cx[t, 0, 2 * d + b, first : first + count]), 0, level, t)
 
     def guest_q(t, level):
         first, count, _ = REGIONS[level]
@@ -266,16 +292,16 @@
     def own_kv(t, level):
         first, count, _ = REGIONS[level]
         span = slice(first, first + count)
-        k = join(lambda d, b: ck[t, 2 * d + b, span])
+        k = join(lambda d, b: cx[t, 1, 2 * d + b, span])
         kd = join(lambda d, b: dks[d, t, span, b * DIM : (b + 1) * DIM])
-        return jnp.concatenate([k, kd], axis=1), join(lambda d, b: cv[t, 2 * d + b, span])
+        return jnp.concatenate([k, kd], axis=1), join(lambda d, b: cx[t, 2, 2 * d + b, span])
 
     def both_kv(t, level):
         first, count, _ = REGIONS[level]
         span = slice(first - 192, first - 192 + count)
-        k = join(lambda d, b: kp[t, 2 * d + b, span])
+        k = join(lambda d, b: kvp[t, 0, 2 * d + b, span])
         kd = join(lambda d, b: dps[d, t, span, b * DIM : (b + 1) * DIM])
-        v = join(lambda d, b: vp[t, 2 * d + b, span])
+        v = join(lambda d, b: kvp[t, 1, 2 * d + b, span])
         own_k, own_v = own_kv(t, level)
         return (
             jnp.concatenate([own_k, jnp.concatenate([k, kd], axis=1)], axis=0),
@@ -304,18 +330,26 @@
     def partner_out(t):
         return remote(
             ob.at[1 - j, t, :, pl.ds(0, SEL)], oo_in.at[t, :, pl.ds(0, SEL)],
-            oo_send.at[t], oo_recv.at[t], device(0, 1 - j),
+            oo_send, oo_recv, device(0, 1 - j),
         )
 
-    def ret_copy(t, piece, low, high, d):
+    def ret_copy(t, low, high, d):
         return remote(
             os1.at[d, t, :, pl.ds(low, high - low)], far_out.at[HALF * j + t, :, pl.ds(low, high - low)],
-            o_send.at[d, piece, t], o_recv.at[j, piece, t], device(1, d),
+            o_send, o_recv, device(1, d),
         )
 
-    def own_head(t, _):
-        for copy in exchange(t):
-            copy.wait_recv()
+    plans = (
+        (c == 0, "2", ""),
+        (c == 1, "34", "34"),
+        (c == 5, "34", "3"),
+        (c % 4 == 2, "234", ""),
+        (c == 3, "4", ""),
+        (c == 4, "24", ""),
+    )
+
+    def level_head(t, _):
+        exchange(t).wait_recv()
         pick = pbuf[t]
         dqs[t] = nt(pick, ot_q[...]).astype(BF16)
         for d in range(2):
@@ -331,7 +365,7 @@
         for level in (1, 2, 3):
             problems.append((own_q(t, level),) + own_kv(t, level) + (near(4 * REGIONS[level][1]),))
         for h in (2 * t, 2 * t + 1):
-            q, k, v = columns(qv, h), columns(kv, h), columns(vv, h)
+            q, k, v = columns(0, h), columns(1, h), columns(2, h)
             for b in range(2):
                 span = slice(b * CHUNK, (b + 1) * CHUNK)
                 problems.append((q[span], k[span], v[span], lambda s, b=b: s + bias0[b]))
@@ -345,36 +379,18 @@
                 o, lse = results[5 + 2 * i + b]
                 o0[2 * t + i, span] = o
                 keep(lse0, (), span, 2 * t + i, lse)
-        return 0
-
-    lax.fori_loop(0, HALF, own_head, 0)
-
-    plans = (
-        (c == 0, "2", ""),
-        (c == 1, "34", "34"),
-        (c == 5, "34", "3"),
-        (c % 4 == 2, "234", ""),
-        (c == 3, "4", ""),
-        (c == 4, "24", ""),
-    )
-
-    def guest_head(t, _):
-        for present, pieces in next_pieces(c - 1):
+
+        for present, (low, high) in next_pieces(c - 1):
 
             @pl.when(present & (c >= 1))
             def _():
-                for low, high in pieces:
-                    for d in range(2):
-                        for copy in kv_copies(t, 0, low, high, d):
-                            copy.wait_recv()
+                got(kvp.at[t, :, :, pl.ds(low, high - low)], k_recv.at[t])
 
         for present, pieces in far_pieces(c + 1):
 
             @pl.when(present & (c <= 6))
             def _():
-                for piece, (low, high) in enumerate(pieces):
-                    for d in range(2):
-                        q_copy(t, 0, piece, low, high, d).wait_recv()
+                got(q1in.at[t, :, pl.ds(0, size_of(pieces))], q_recv.at[t])
 
         for present, guests, owns in plans:
 
@@ -399,14 +415,14 @@
 
             @pl.when(present & (c <= 6))
             def _():
-                for piece, (low, high) in enumerate(pieces):
+                for low, high in pieces:
                     for d in range(2):
-                        ret_copy(t, piece, low, high, d).start()
+                        ret_copy(t, low, high, d).start()
 
         partner_out(t).start()
         return 0
 
-    lax.fori_loop(0, HALF, guest_head, 0)
+    lax.fori_loop(0, HALF, level_head, 0)
 
     for d in range(2):
         for b in range(2):
@@ -414,14 +430,14 @@
             ls_own[d, b] = st_own[d, b].T[:HALF]
 
     def far_stats(d):
-        return remote(ls1.at[d], lsef_out.at[j], l_send.at[1 + d], l_recv.at[1 + j], device(1, d))
+        return remote(ls1.at[d], lsef_out.at[j], l_send, l_recv.at[1 + j], device(1, d))
 
     @pl.when(c <= 6)
     def _():
         for d in range(2):
             far_stats(d).start()
 
-    l_own = remote(ls_own.at[1 - j], lo_in, l_send.at[0], l_recv.at[0], device(0, 1 - j))
+    l_own = remote(ls_own.at[1 - j], lo_in, l_own_send, l_recv.at[0], device(0, 1 - j))
     l_own.start()
     l_own.wait_recv()
 
@@ -448,21 +464,22 @@
         back = back + fold3(nt(split3(jnp.where(chosen[level], lse, 0.0)), spread[level]))
     al_own[...] = jnp.exp2(own - back)
     lse_loc[...] = lse
-    lse_copy = pltpu.make_async_copy(lse_loc, lse_out, lse_sem.at[0])
+    lse_copy = pltpu.make_async_copy(lse_loc, lse_out, lse_sem)
     lse_copy.start()
     for b in range(2):
         span = slice(b * CHUNK, (b + 1) * CHUNK)
         a0[span] = jnp.exp2(lse0[span] - upright(lse, b))
 
     def loc_copy(h):
-        return pltpu.make_async_copy(loc.at[h], loc_out.at[h], store_sem.at[h])
+        return pltpu.make_async_copy(loc.at[h], loc_out.at[h], store_sem)
 
     own_first = jnp.where(wide < 128, 0, jnp.where(wide < 192, 128, jnp.where(wide < 224, 192, 224)))
     own_bits = jnp.where(wide < 128, 1, jnp.where(wide < 192, 2, jnp.where(wide < 224, 3, 4)))
     own_base = tall - ((wide - own_first) << own_bits)
 
+    got(oo_in.at[:, :, pl.ds(0, SEL)], oo_recv)
+
     def local_head(t, _):
-        partner_out(t).wait_recv()
         for which in range(2):
             h = HALF * j + t if which == 0 else HALF * (1 - j) + t
             o1, o2, o3, o4 = [off_ref[i, h] & (2 << i) - 1 for i in range(4)]
@@ -479,58 +496,45 @@
 
     lax.fori_loop(0, HALF, local_head, 0)
 
-    for copy in docs_copies:
-        copy.wait_send()
+    for present, slots in ((near_chips[0][1] & near_chips[1][1], 5), (c == 0, 3), (c == 7, 3)):
+
+        @pl.when(present)
+        def _():
+            part = docs_all.at[pl.ds(0, slots)]
+            remote(part, part, d_send, d_recv.at[0], device(0, 1 - j)).wait_send()
+
     l_own.wait_send()
     lse_copy.wait()
 
-    def drain(t, _):
-        for which in range(2):
-            each_q(t, which, lambda copy: copy.wait_send())
-            each_kv(t, which, lambda copy: copy.wait_send())
-        for copy in exchange(t):
-            copy.wait_send()
-        partner_out(t).wait_send()
-        loc_copy(2 * t).wait()
-        loc_copy(2 * t + 1).wait()
-        return 0
-
-    lax.fori_loop(0, HALF, drain, 0)
-
-    def drain_far(t, _):
-        for present, pieces in far_pieces(c + 1):
-
-            @pl.when(present & (c <= 6))
-            def _():
-                for piece, (low, high) in enumerate(pieces):
-                    for d in range(2):
-                        ret_copy(t, piece, low, high, d).wait_send()
-
-        for present, pieces in far_pieces(c):
-
-            @pl.when(present)
-            def _():
-                for piece, (low, high) in enumerate(pieces):
-                    for i in range(2):
-                        remote(
-                            os1.at[0, t, :, pl.ds(low, high - low)],
-                            far_out.at[HALF * i + t, :, pl.ds(low, high - low)],
-                            o_send.at[0, piece, t], o_recv.at[i, piece, t], device(1, 0),
-                        ).wait_recv()
-
-        return 0
-
-    lax.fori_loop(0, HALF, drain_far, 0)
-
-    @pl.when(c <= 6)
-    def _():
-        for d in range(2):
-            far_stats(d).wait_send()
-
-    @pl.when(c >= 1)
-    def _():
-        for i in range(2):
-            remote(ls1.at[0], lsef_out.at[i], l_send.at[1], l_recv.at[1 + i], device(1, 0)).wait_recv()
+    sent(sx, x_send)
+    sent(oo_in.at[:, :, pl.ds(0, SEL)], oo_send)
+    pltpu.make_async_copy(loc, loc_out, store_sem).wait()
+    for present, pieces in far_pieces(c):
+
+        @pl.when(present)
+        def _():
+            sent(q1in.at[:, :, pl.ds(0, size_of(pieces))], q_send)
+
+    for present, (low, high) in next_pieces(c):
+
+        @pl.when(present)
+        def _():
+            sent(kvp.at[:, :, :, pl.ds(0, high - low)], k_send)
+
+    for present, pieces in far_pieces(c + 1):
+
+        @pl.when(present & (c <= 6))
+        def _():
+            sent(os1.at[:, :, :, pl.ds(0, size_of(pieces))], o_send)
+            sent(ls1, l_send)
+
+    for present, pieces in far_pieces(c):
+
+        @pl.when(present)
+        def _():
+            got(far_out.at[:, :, pl.ds(0, size_of(pieces))], o_recv)
+            for i in range(2):
+                got(lsef_out.at[i], l_recv.at[1 + i])
 
 
 def picked(off_ref, level, bits):
@@ -557,7 +561,7 @@
     return jnp.concatenate([dense[b * HEADS : (b + 1) * HEADS], pad], axis=0).T
 
 
-GROUP = 4
+GROUP = 8
 
 
 def join_kernel(loc_ref, far_ref, lse_ref, lsef_ref, off_ref, out_ref, al_far, a_loc):
@@ -622,13 +626,11 @@
             jax.ShapeDtypeStruct((2 * HEADS, CHUNK), F32),
             jax.ShapeDtypeStruct((2, 2, HALF, DIM), F32),
         ),
-        in_specs=[any_space, any_space, any_space, pl.BlockSpec(memory_space=pltpu.VMEM), smem],
+        in_specs=[any_space] * 5,
         out_specs=(any_space,) * 4,
         scratch_shapes=[
-            vmem(ROWS, HEADS * DIM), vmem(ROWS, HEADS * DIM), vmem(ROWS, HEADS * DIM),
-            vmem(HALF, 4, SEL, DIM), vmem(HALF, 4, SEL, DIM), vmem(HALF, 4, SEL, DIM),
-            vmem(HALF, 2, SEL, DIM), vmem(HALF, 2, SEL, DIM), vmem(HALF, 2, SEL, DIM),
-            vmem(HALF, 4, FAR, DIM), vmem(HALF, 4, FAR3, DIM), vmem(HALF, 4, FAR3, DIM),
+            vmem(1, ROWS, kind=I32), pltpu.SMEM((4, HEADS), I32), vmem(3, ROWS, HEADS * DIM),
+            vmem(HALF, 3, 4, SEL, DIM), vmem(HALF, 3, 2, SEL, DIM), vmem(HALF, 4, FAR, DIM), vmem(HALF, 2, 4, FAR3, DIM),
             vmem(HALF, SEL, CHUNK), vmem(2, HALF, SEL, CHUNK), vmem(2, HALF, FAR3, CHUNK), vmem(HALF, SEL, CHUNK),
             vmem(2, HALF, 2, CHUNK, DIM), vmem(HALF, 2, CHUNK, DIM), vmem(2, HALF, 2, FAR, DIM),
             vmem(HEADS, ROWS, DIM, kind=F32), vmem(HEADS, ROWS, DIM),
@@ -638,9 +640,7 @@
             vmem(6, 1, ROWS, kind=I32), vmem(2 * DIM, CHUNK), vmem(4, 2 * DIM, CHUNK),
             vmem(SEL, CHUNK, kind=I32), vmem(CHUNK, CHUNK, kind=F32), vmem(2, CHUNK, CHUNK, kind=F32),
             vmem(2 * HEADS, CHUNK, kind=F32), vmem(ROWS, DIM, kind=F32),
-            dma((4, 2, 3)), dma((HEADS,)), dma((1,)), dma((5,)), dma((6,)), dma((3, HALF)), dma((3, HALF)),
-            dma((2, 2, HALF)), dma((2, 2, HALF)), dma((2, HALF)), dma((2, HALF)), dma((2, HALF)), dma((2, HALF)),
-            dma((2, 2, HALF)), dma((2, 2, HALF)), dma((HALF,)), dma((HALF,)), dma((3,)), dma((3,)),
+            dma((6,)), dma((12,)), dma((6,)), dma((HALF,)), dma((HALF,)), dma((HALF,)), dma((3,)),
         ],
         compiler_params=pltpu.CompilerParams(collective_id=0, has_side_effects=True, vmem_limit_bytes=56 << 20),
         name="dilated_attention",

time: 51.5 us -> 41.4 us (0.80)
  the two profiles are of different devices: /device:TPU:25 before, /device:TPU:111 now
where the time goes in v1:
time: 41.4 us; the launch traced here: 41.3 us
  Pallas kernels  41.3 us (100%)
    pallas_call x1, Pallas kernels, on_device(): pl.pallas_call(kernel, out_shape=(jax.ShapeDtypeStruct((HEADS, ROWS, DIM)...  37 us
    pallas_call x1, Pallas kernels, on_device(): pl.pallas_call(join_kernel, grid=(HEADS // GROUP,), out_shape=jax.ShapeDt...  4.24 us

profile of v1, /device:TPU:111, one launch (start us, length us, event | category | flops | bytes accessed | tf_op | source)
XLA Modules:
  0.0 41.3 jit_solution(14701304061300747139)
XLA Ops:
  0.0 37.0 %dilated_attention.1 = (bf16[16,512,128]{2,1,0:T(8,128)(2,1)}, bf16[16,2,128,128]{3,2,1,0:T(8,128)(2,1)}, f32[32,256]{1,0:T(8,128)}, f32[2,2,8,128]{3,2,1,0:T(8,128)}) custom-call(bf16[1,512,2048]{2,1,0:T(8,128)(2,1)} %q_hbm.1, bf16[1,512,2048]{2,1,0:T(8,128)(2,1)} %k_hbm.1, bf16[1,512,2048]{2,1,0:T(8,128)(2,1)} %v_hbm.1, s32[1,512]{1,0:T(1,128)} %docs_hbm.1, ...), custom_call_target="tpu_custom_call" | custom-call | tf_op jit(solution)/shard_map/dilated_attention/pallas_call | solution.py:621
  37.0 4.2 %join_far.1 = bf16[1,512,2048]{2,1,0:T(8,128)(2,1)} custom-call(bf16[16,512,128]{2,1,0:T(8,128)(2,1)} %get-tuple-element.9.loc_ref, bf16[16,2,128,128]{3,2,1,0:T(8,128)(2,1)} %get-tuple-element.10.far_ref, f32[32,256]{1,0:T(8,128)} %get-tuple-element.11.lse_ref, f32[2,2,8,128]{3,2,1,0:T(8,128)} %get-tuple-element.12.lsef_ref, s32[4,16]{1,0:T(4,128)} %off_ref.1), custom_call_target="tpu_custom_call" | custom-call | tf_op jit(solution)/shard_map/join_far/pallas_call | solution.py:648

commit v2 on v1

--- a/solution.py
+++ b/solution.py
@@ -53,22 +53,21 @@
     return (
         (chip % 4 == 3, ((0, FAR),)),
         (chip % 4 == 2, ((64, FAR),)),
-        (chip == 1, ((0, 64),)),
-        (chip == 5, ((0, 64), (96, FAR))),
+        (chip % 4 == 1, ((0, 64),)),
         (chip == 4, ((96, FAR),)),
     )
 
 
 def next_pieces(chip):
-    return ((chip % 4 < 2, (0, FAR3)), ((chip == 2) | (chip == 3), (32, FAR3)))
+    return ((chip % 4 < 2, (0, FAR3)), (chip == 2, (32, FAR3)))
 
 
 def kernel(
     q_hbm, k_hbm, v_hbm, docs_hbm, off_hbm,
-    loc_out, far_out, lse_out, lsef_out,
-    docs_ref, off_ref, xv, cx, sx, q1in, kvp, dqs, dks, dps, pbuf,
-    ob, oo_in, os1, o0, loc,
-    st_own, st1, lse0, ls_own, ls1, lo_in, lse_loc,
+    loc_out, far_out, lse_out, lsef_out, lsef2_out,
+    docs_ref, off_ref, xv, cx, sx, q1in, q2in, kvp, dqs, dks, dps, pbuf,
+    ob, oo_in, os1, os2, o0, loc,
+    st_own, st1, st2, lse0, ls_own, ls1, ls2, lo_in, lse_loc,
     docs_all, ot_q, ot_k, base_m, causal, bias0, al_own, a0,
     load_sem, once, d_recv, x_recv, q_recv, k_recv, l_recv,
 ):
@@ -85,8 +84,8 @@
             src_ref=src, dst_ref=dst, send_sem=send, recv_sem=recv, device_id=to, device_id_type=MESH
         )
 
-    store_sem, lse_sem, d_send, x_send, q_send, k_send, o_send, o_recv, oo_send, oo_recv, l_send, l_own_send = [
-        once.at[i] for i in range(12)
+    store_sem, lse_sem, d_send, x_send, q_send, k_send, o_send, o_recv, oo_send, oo_recv, l_send, l_own_send, two_send, two_recv, o_two_send, o_two_recv, l_two_send = [
+        once.at[i] for i in range(17)
     ]
 
     def load_start(u):
@@ -120,9 +119,17 @@
             for core in (0, 1):
                 pl.semaphore_signal(barrier, inc=1, device_id=device(g, core), device_id_type=MESH)
 
+    guest_of_two = ((c == 5, -2), (c == 3, 2))
+    for present, g in guest_of_two:
+
+        @pl.when(present)
+        def _():
+            for core in (0, 1):
+                pl.semaphore_signal(barrier, inc=1, device_id=device(g, core), device_id_type=MESH)
+
     docs_load.wait()
     off_load.wait()
-    pl.semaphore_wait(barrier, 1 + jnp.where(c <= 6, 2, 0) + jnp.where(c >= 1, 2, 0))
+    pl.semaphore_wait(barrier, 1 + jnp.where(c <= 6, 2, 0) + jnp.where(c >= 1, 2, 0) + jnp.where((c == 3) | (c == 5), 2, 0))
 
     def docs_copy(g, core, slot):
         return remote(docs_ref, docs_all.at[slot], d_send, d_recv.at[slot], device(g, core))
@@ -135,6 +142,11 @@
             def _():
                 for core in (0, 1):
                     do(docs_copy(g, core, first + j))
+
+        @pl.when(c == 5)
+        def _():
+            for core in (0, 1):
+                do(docs_copy(-2, core, 6 + j))
 
     each_docs(lambda copy: copy.start())
     docs_all[j] = docs_ref[...]
@@ -158,7 +170,18 @@
             k_send, k_recv.at[t], device(1, core_of(which)),
         )
 
+    def two_copy(t, which):
+        rows = pl.ds(224, 16)
+        return remote(
+            sx.at[t, 0, :, rows] if which == 0 else cx.at[t, 0, pl.ds(2 * j, 2), rows],
+            q2in.at[t, pl.ds(2 * j, 2)], two_send, two_recv, device(-2, core_of(which)),
+        )
+
     def each_q(t, which):
+        @pl.when(c == 5)
+        def _():
+            two_copy(t, which).start()
+
         for present, pieces in far_pieces(c):
 
             @pl.when(present)
@@ -254,10 +277,20 @@
             for core in (0, 1):
                 docs_all[first + core] = docs_ref[...]
 
+    @pl.when(c == 3)
+    def _():
+        for core in (0, 1):
+            docs_copy(-2, core, 6 + core).wait_recv()
+
+    @pl.when(c != 3)
+    def _():
+        for core in (0, 1):
+            docs_all[6 + core] = docs_ref[...]
+
     for b in range(2):
         span = slice(b * CHUNK, (b + 1) * CHUNK)
-        ones = [jnp.where(docs_all[g, :, span] == iota((8, CHUNK), 0), 1.0, 0.0) for g in range(4)]
-        ones.append(jnp.zeros((DIM - 32, CHUNK), F32))
+        ones = [jnp.where(docs_all[g, :, span] == iota((8, CHUNK), 0), 1.0, 0.0) for g in (0, 1, 2, 3, 6, 7)]
+        ones.append(jnp.zeros((DIM - 48, CHUNK), F32))
         ot_q[b * DIM : (b + 1) * DIM] = jnp.concatenate(ones, axis=0).astype(BF16)
         for i, slot in enumerate((0, 1, 4, 5)):
             same = docs_all[slot, :, span] == (iota((DIM, CHUNK), 0) & 7)
@@ -340,12 +373,10 @@
         )
 
     plans = (
-        (c == 0, "2", ""),
-        (c == 1, "34", "34"),
-        (c == 5, "34", "3"),
+        (c % 4 == 0, "2", ""),
+        (c % 4 == 1, "34", "34"),
         (c % 4 == 2, "234", ""),
         (c == 3, "4", ""),
-        (c == 4, "24", ""),
     )
 
     def level_head(t, _):
@@ -423,6 +454,35 @@
         return 0
 
     lax.fori_loop(0, HALF, level_head, 0)
+
+    def two_back(d):
+        return remote(
+            os2.at[d], far_out.at[pl.ds(pl.multiple_of(HALF * j, HALF), HALF), :, pl.ds(96, 16)],
+            o_two_send, o_two_recv, device(2, d),
+        )
+
+    def two_stats(d):
+        return remote(ls2.at[d], lsef2_out.at[j], l_two_send, l_recv.at[3 + j], device(2, d))
+
+    @pl.when(c == 3)
+    def _():
+        got(q2in, two_recv)
+        problems = []
+        for t in range(HALF):
+            q = with_docs(join(lambda d, b: q2in[t, 2 * d + b]), 2, 3, t)
+            problems.append((q,) + own_kv(t, 3) + (None,))
+        for t, (o, lse) in enumerate(attend(problems)):
+            for d in range(2):
+                for b in range(2):
+                    rows = slice((2 * d + b) * 16, (2 * d + b + 1) * 16)
+                    os2[d, t, b] = o[rows].astype(BF16)
+                    keep(st2, (d, b), slice(96, FAR), t, lse[rows])
+        for d in range(2):
+            for b in range(2):
+                ls2[d, b] = st2[d, b].T[:HALF]
+        for d in range(2):
+            two_back(d).start()
+            two_stats(d).start()
 
     for d in range(2):
         for b in range(2):
@@ -496,7 +556,7 @@
 
     lax.fori_loop(0, HALF, local_head, 0)
 
-    for present, slots in ((near_chips[0][1] & near_chips[1][1], 5), (c == 0, 3), (c == 7, 3)):
+    for present, slots in (((c > 0) & (c < 7) & (c != 5), 5), ((c == 0) | (c == 7), 3), (c == 5, 7)):
 
         @pl.when(present)
         def _():
@@ -527,6 +587,18 @@
         def _():
             sent(os1.at[:, :, :, pl.ds(0, size_of(pieces))], o_send)
             sent(ls1, l_send)
+
+    @pl.when(c == 3)
+    def _():
+        sent(os2, o_two_send)
+        sent(ls2, l_two_send)
+
+    @pl.when(c == 5)
+    def _():
+        sent(q2in, two_send)
+        got(far_out.at[:, :, pl.ds(0, 16)], o_two_recv)
+        for i in range(2):
+            got(lsef2_out.at[i], l_recv.at[3 + i])
 
     for present, pieces in far_pieces(c):
 
@@ -564,7 +636,7 @@
 GROUP = 8
 
 
-def join_kernel(loc_ref, far_ref, lse_ref, lsef_ref, off_ref, out_ref, al_far, a_loc):
+def join_kernel(loc_ref, far_ref, lse_ref, lsef_ref, lsef2_ref, off_ref, out_ref, al_far, a_loc):
     c = lax.axis_index("ctx") // 2
     lane = iota((1, DIM), 1)
 
@@ -573,7 +645,10 @@
 
     @pl.when(pl.program_id(0) == 0)
     def _():
-        far = jnp.concatenate([lsef_ref[0, 0], lsef_ref[1, 0], lsef_ref[0, 1], lsef_ref[1, 1]], axis=0)
+        one, two = [
+            jnp.concatenate([ref[0, 0], ref[1, 0], ref[0, 1], ref[1, 1]], axis=0) for ref in (lsef_ref, lsef2_ref)
+        ]
+        far = jnp.where((lane >= 96) & (c == 5), two, one)
         far = jnp.where(valid(lane), far, NEG)
         far3 = split3(far)
         tall = iota((DIM, CHUNK), 0) + DIM
@@ -618,29 +693,33 @@
     def vmem(*shape, kind=BF16):
         return pltpu.VMEM(shape, kind)
 
-    local, far, lse, lse_far = pl.pallas_call(
+    local, far, lse, lse_far, lse_far2 = pl.pallas_call(
         kernel,
         out_shape=(
             jax.ShapeDtypeStruct((HEADS, ROWS, DIM), BF16),
             jax.ShapeDtypeStruct((HEADS, 2, DIM, DIM), BF16),
             jax.ShapeDtypeStruct((2 * HEADS, CHUNK), F32),
             jax.ShapeDtypeStruct((2, 2, HALF, DIM), F32),
+            jax.ShapeDtypeStruct((2, 2, HALF, DIM), F32),
         ),
         in_specs=[any_space] * 5,
-        out_specs=(any_space,) * 4,
+        out_specs=(any_space,) * 5,
         scratch_shapes=[
             vmem(1, ROWS, kind=I32), pltpu.SMEM((4, HEADS), I32), vmem(3, ROWS, HEADS * DIM),
-            vmem(HALF, 3, 4, SEL, DIM), vmem(HALF, 3, 2, SEL, DIM), vmem(HALF, 4, FAR, DIM), vmem(HALF, 2, 4, FAR3, DIM),
+            vmem(HALF, 3, 4, SEL, DIM), vmem(HALF, 3, 2, SEL, DIM), vmem(HALF, 4, FAR, DIM), vmem(HALF, 4, 16, DIM),
+            vmem(HALF, 2, 4, FAR3, DIM),
             vmem(HALF, SEL, CHUNK), vmem(2, HALF, SEL, CHUNK), vmem(2, HALF, FAR3, CHUNK), vmem(HALF, SEL, CHUNK),
-            vmem(2, HALF, 2, CHUNK, DIM), vmem(HALF, 2, CHUNK, DIM), vmem(2, HALF, 2, FAR, DIM),
+            vmem(2, HALF, 2, CHUNK, DIM), vmem(HALF, 2, CHUNK, DIM), vmem(2, HALF, 2, FAR, DIM), vmem(2, HALF, 2, 16, DIM),
             vmem(HEADS, ROWS, DIM, kind=F32), vmem(HEADS, ROWS, DIM),
-            vmem(2, 2, CHUNK, DIM, kind=F32), vmem(2, 2, DIM, DIM, kind=F32), vmem(ROWS, DIM, kind=F32),
-            vmem(2, 2, HALF, CHUNK, kind=F32), vmem(2, 2, HALF, DIM, kind=F32), vmem(2, HALF, CHUNK, kind=F32),
+            vmem(2, 2, CHUNK, DIM, kind=F32), vmem(2, 2, DIM, DIM, kind=F32), vmem(2, 2, DIM, DIM, kind=F32),
+            vmem(ROWS, DIM, kind=F32),
+            vmem(2, 2, HALF, CHUNK, kind=F32), vmem(2, 2, HALF, DIM, kind=F32), vmem(2, 2, HALF, DIM, kind=F32),
+            vmem(2, HALF, CHUNK, kind=F32),
             vmem(2 * HEADS, CHUNK, kind=F32),
-            vmem(6, 1, ROWS, kind=I32), vmem(2 * DIM, CHUNK), vmem(4, 2 * DIM, CHUNK),
+            vmem(8, 1, ROWS, kind=I32), vmem(2 * DIM, CHUNK), vmem(4, 2 * DIM, CHUNK),
             vmem(SEL, CHUNK, kind=I32), vmem(CHUNK, CHUNK, kind=F32), vmem(2, CHUNK, CHUNK, kind=F32),
             vmem(2 * HEADS, CHUNK, kind=F32), vmem(ROWS, DIM, kind=F32),
-            dma((6,)), dma((12,)), dma((6,)), dma((HALF,)), dma((HALF,)), dma((HALF,)), dma((3,)),
+            dma((6,)), dma((17,)), dma((8,)), dma((HALF,)), dma((HALF,)), dma((HALF,)), dma((5,)),
         ],
         compiler_params=pltpu.CompilerParams(collective_id=0, has_side_effects=True, vmem_limit_bytes=56 << 20),
         name="dilated_attention",
@@ -654,13 +733,14 @@
             pl.BlockSpec((GROUP, 2, DIM, DIM), lambda i: (i, 0, 0, 0)),
             pl.BlockSpec(memory_space=pltpu.VMEM),
             pl.BlockSpec(memory_space=pltpu.VMEM),
+            pl.BlockSpec(memory_space=pltpu.VMEM),
             smem,
         ],
         out_specs=pl.BlockSpec((1, ROWS, GROUP * DIM), lambda i: (0, 0, i)),
         scratch_shapes=[vmem(2 * HEADS, DIM, kind=F32), vmem(ROWS, DIM, kind=F32)],
         compiler_params=pltpu.CompilerParams(vmem_limit_bytes=60 << 20),
         name="join_far",
-    )(local, far, lse, lse_far, dilation_offsets)
+    )(local, far, lse, lse_far, lse_far2, dilation_offsets)
 
 
 def solution(mesh):

time: 41.4 us -> 38.7 us (0.935)
  Pallas kernels: 41.3 us -> 38.5 us
    pallas_call x1, Pallas kernels: 37 us -> 34.3 us  [on_device(): pl.pallas_call(kernel, out_shape=(jax.ShapeDtypeStruct((HEADS, ROWS, DIM)...]
where the time goes in v2:
time: 38.7 us; the launch traced here: 38.5 us
  Pallas kernels  38.5 us (99%)
    pallas_call x1, Pallas kernels, on_device(): pl.pallas_call(kernel, out_shape=(jax.ShapeDtypeStruct((HEADS, ROWS, DIM)...  34.3 us
    pallas_call x1, Pallas kernels, on_device(): pl.pallas_call(join_kernel, grid=(HEADS // GROUP,), out_shape=jax.ShapeDt...  4.25 us

profile of v2, /device:TPU:111, one launch (start us, length us, event | category | flops | bytes accessed | tf_op | source)
XLA Modules:
  0.0 38.5 jit_solution(5934151381984567086)
XLA Ops:
  0.0 34.3 %dilated_attention.1 = (bf16[16,512,128]{2,1,0:T(8,128)(2,1)}, bf16[16,2,128,128]{3,2,1,0:T(8,128)(2,1)}, f32[32,256]{1,0:T(8,128)}, f32[2,2,8,128]{3,2,1,0:T(8,128)}, f32[2,2,8,128]{3,2,1,0:T(8,128)}) custom-call(bf16[1,512,2048]{2,1,0:T(8,128)(2,1)} %q_hbm.1, bf16[1,512,2048]{2,1,0:T(8,128)(2,1)} %k_hbm.1, bf16[1,512,2048]{2,1,0:T(8,128)(2,1)} %v_hbm.1, ...), custom_call_target="tpu_custom_call" | custom-call | tf_op jit(solution)/shard_map/dilated_attention/pallas_call | solution.py:696
  34.3 4.2 %join_far.1 = bf16[1,512,2048]{2,1,0:T(8,128)(2,1)} custom-call(bf16[16,512,128]{2,1,0:T(8,128)(2,1)} %get-tuple-element.10.loc_ref, bf16[16,2,128,128]{3,2,1,0:T(8,128)(2,1)} %get-tuple-element.11.far_ref, f32[32,256]{1,0:T(8,128)} %get-tuple-element.12.lse_ref, f32[2,2,8,128]{3,2,1,0:T(8,128)} %get-tuple-element.13.lsef_ref, ...), custom_call_target="tpu_custom_call" | custom-call | tf_op jit(solution)/shard_map/join_far/pallas_call | solution.py:727

commit v3 on v2

--- a/solution.py
+++ b/solution.py
@@ -64,11 +64,11 @@
 
 def kernel(
     q_hbm, k_hbm, v_hbm, docs_hbm, off_hbm,
-    loc_out, far_out, lse_out, lsef_out, lsef2_out,
+    loc_out, far_out, al_out, share_out,
     docs_ref, off_ref, xv, cx, sx, q1in, q2in, kvp, dqs, dks, dps, pbuf,
     ob, oo_in, os1, os2, o0, loc,
-    st_own, st1, st2, lse0, ls_own, ls1, ls2, lo_in, lse_loc,
-    docs_all, ot_q, ot_k, base_m, causal, bias0, al_own, a0,
+    st_own, st1, st2, lse0, ls_own, ls1, ls2, lo_in, lr1, lr2, lse_loc,
+    docs_all, ot_q, ot_k, base_m, causal, bias0, al_own, a0, al_far, share,
     load_sem, once, d_recv, x_recv, q_recv, k_recv, l_recv,
 ):
     me = lax.axis_index("ctx")
@@ -84,9 +84,27 @@
             src_ref=src, dst_ref=dst, send_sem=send, recv_sem=recv, device_id=to, device_id_type=MESH
         )
 
-    store_sem, lse_sem, d_send, x_send, q_send, k_send, o_send, o_recv, oo_send, oo_recv, l_send, l_own_send, two_send, two_recv, o_two_send, o_two_recv, l_two_send = [
-        once.at[i] for i in range(17)
+    store_sem, lse_sem, d_send, x_send, q_send, k_send, o_send, o_recv, oo_send, oo_recv, l_send, l_own_send, two_send, two_recv, o_two_send, o_two_recv, l_two_send, al_sem = [
+        once.at[i] for i in range(18)
     ]
+
+    near_chips = ((1, c <= 6), (-1, c >= 1))
+    barrier = pltpu.get_barrier_semaphore()
+    pl.semaphore_signal(barrier, inc=1, device_id=device(0, 1 - j), device_id_type=MESH)
+    for g, present in near_chips:
+
+        @pl.when(present)
+        def _():
+            for core in (0, 1):
+                pl.semaphore_signal(barrier, inc=1, device_id=device(g, core), device_id_type=MESH)
+
+    guest_of_two = ((c == 5, -2), (c == 3, 2))
+    for present, g in guest_of_two:
+
+        @pl.when(present)
+        def _():
+            for core in (0, 1):
+                pl.semaphore_signal(barrier, inc=1, device_id=device(g, core), device_id_type=MESH)
 
     def load_start(u):
         for half in range(2):
@@ -108,24 +126,6 @@
 
     for first, count, bits in REGIONS:
         base_m[first : first + count] = iota((count, CHUNK), 1) - (iota((count, CHUNK), 0) << bits)
-
-    near_chips = ((1, c <= 6), (-1, c >= 1))
-    barrier = pltpu.get_barrier_semaphore()
-    pl.semaphore_signal(barrier, inc=1, device_id=device(0, 1 - j), device_id_type=MESH)
-    for g, present in near_chips:
-
-        @pl.when(present)
-        def _():
-            for core in (0, 1):
-                pl.semaphore_signal(barrier, inc=1, device_id=device(g, core), device_id_type=MESH)
-
-    guest_of_two = ((c == 5, -2), (c == 3, 2))
-    for present, g in guest_of_two:
-
-        @pl.when(present)
-        def _():
-            for core in (0, 1):
-                pl.semaphore_signal(barrier, inc=1, device_id=device(g, core), device_id_type=MESH)
 
     docs_load.wait()
     off_load.wait()
@@ -378,6 +378,15 @@
         (c % 4 == 2, "234", ""),
         (c == 3, "4", ""),
     )
+
+    def each_return(t, more):
+        for present, pieces in far_pieces(c + 1):
+
+            @pl.when(present & (c <= 6) & more)
+            def _():
+                for low, high in pieces:
+                    for d in range(2):
+                        ret_copy(t, low, high, d).start()
 
     def level_head(t, _):
         exchange(t).wait_recv()
@@ -442,18 +451,28 @@
                 for name, result in zip(owns, results[len(guests) :]):
                     put(t, int(name) - 1, result, ob, st_own, 0)
 
-        for present, pieces in far_pieces(c + 1):
-
-            @pl.when(present & (c <= 6))
-            def _():
-                for low, high in pieces:
-                    for d in range(2):
-                        ret_copy(t, low, high, d).start()
-
+        each_return(t, t < HALF - jnp.where(c % 4 == 0, 3, 1))
         partner_out(t).start()
         return 0
 
     lax.fori_loop(0, HALF, level_head, 0)
+
+    for d in range(2):
+        for b in range(2):
+            ls1[d, b] = st1[d, b].T[:HALF]
+            ls_own[d, b] = st_own[d, b].T[:HALF]
+
+    def far_stats(d):
+        return remote(ls1.at[d], lr1.at[j], l_send, l_recv.at[1 + j], device(1, d))
+
+    @pl.when(c <= 6)
+    def _():
+        for d in range(2):
+            far_stats(d).start()
+
+    each_return(HALF - 3, c % 4 == 0)
+    each_return(HALF - 2, c % 4 == 0)
+    each_return(HALF - 1, True)
 
     def two_back(d):
         return remote(
@@ -462,7 +481,7 @@
         )
 
     def two_stats(d):
-        return remote(ls2.at[d], lsef2_out.at[j], l_two_send, l_recv.at[3 + j], device(2, d))
+        return remote(ls2.at[d], lr2.at[j], l_two_send, l_recv.at[3 + j], device(2, d))
 
     @pl.when(c == 3)
     def _():
@@ -481,21 +500,9 @@
             for b in range(2):
                 ls2[d, b] = st2[d, b].T[:HALF]
         for d in range(2):
+            two_stats(d).start()
+        for d in range(2):
             two_back(d).start()
-            two_stats(d).start()
-
-    for d in range(2):
-        for b in range(2):
-            ls1[d, b] = st1[d, b].T[:HALF]
-            ls_own[d, b] = st_own[d, b].T[:HALF]
-
-    def far_stats(d):
-        return remote(ls1.at[d], lsef_out.at[j], l_send, l_recv.at[1 + j], device(1, d))
-
-    @pl.when(c <= 6)
-    def _():
-        for d in range(2):
-            far_stats(d).start()
 
     l_own = remote(ls_own.at[1 - j], lo_in, l_own_send, l_recv.at[0], device(0, 1 - j))
     l_own.start()
@@ -524,8 +531,6 @@
         back = back + fold3(nt(split3(jnp.where(chosen[level], lse, 0.0)), spread[level]))
     al_own[...] = jnp.exp2(own - back)
     lse_loc[...] = lse
-    lse_copy = pltpu.make_async_copy(lse_loc, lse_out, lse_sem)
-    lse_copy.start()
     for b in range(2):
         span = slice(b * CHUNK, (b + 1) * CHUNK)
         a0[span] = jnp.exp2(lse0[span] - upright(lse, b))
@@ -556,6 +561,43 @@
 
     lax.fori_loop(0, HALF, local_head, 0)
 
+    @pl.when(c >= 1)
+    def _():
+        for i in range(2):
+            got(lr1.at[i], l_recv.at[1 + i])
+
+    @pl.when(c == 5)
+    def _():
+        for i in range(2):
+            got(lr2.at[i], l_recv.at[3 + i])
+
+    one, two = [
+        jnp.concatenate([ref[0, 0], ref[1, 0], ref[0, 1], ref[1, 1]], axis=0) for ref in (lr1, lr2)
+    ]
+    far = jnp.where((lane >= 96) & (c == 5), two, one)
+    far = jnp.where(valid_row(lane, c), far, NEG)
+    far3 = split3(far)
+    tall = iota((DIM, CHUNK), 0) + DIM
+    parts, spread, chosen = [lse_loc[...]], [], []
+    for level, (first, count, bits) in enumerate(REGIONS):
+        if level > 0:
+            hit = ((iota((DIM, CHUNK), 1) >> bits) == tall - first) & (tall >= first) & (tall < first + count)
+            spread.append(jnp.where(hit, 1.0, 0.0).astype(BF16))
+            chosen.append(picked(off_ref, level, bits))
+            parts.append(jnp.where(chosen[-1], fold3(nn(far3, spread[-1])), NEG))
+    lse = log_sum(parts)
+    back = jnp.zeros((2 * HEADS, DIM), F32)
+    for pick, wide in zip(chosen, spread):
+        back = back + fold3(nt(split3(jnp.where(pick, lse, 0.0)), wide))
+    al_far[...] = jnp.exp2(far - back)
+    portion = jnp.exp2(lse_loc[...] - lse)
+    for b in range(2):
+        share[b * CHUNK : (b + 1) * CHUNK] = upright(portion, b)
+    al_copy = pltpu.make_async_copy(al_far, al_out, al_sem)
+    share_copy = pltpu.make_async_copy(share, share_out, lse_sem)
+    al_copy.start()
+    share_copy.start()
+
     for present, slots in (((c > 0) & (c < 7) & (c != 5), 5), ((c == 0) | (c == 7), 3), (c == 5, 7)):
 
         @pl.when(present)
@@ -564,8 +606,9 @@
             remote(part, part, d_send, d_recv.at[0], device(0, 1 - j)).wait_send()
 
     l_own.wait_send()
-    lse_copy.wait()
-
+
+    al_copy.wait()
+    share_copy.wait()
     sent(sx, x_send)
     sent(oo_in.at[:, :, pl.ds(0, SEL)], oo_send)
     pltpu.make_async_copy(loc, loc_out, store_sem).wait()
@@ -597,16 +640,16 @@
     def _():
         sent(q2in, two_send)
         got(far_out.at[:, :, pl.ds(0, 16)], o_two_recv)
-        for i in range(2):
-            got(lsef2_out.at[i], l_recv.at[3 + i])
 
     for present, pieces in far_pieces(c):
 
         @pl.when(present)
         def _():
             got(far_out.at[:, :, pl.ds(0, size_of(pieces))], o_recv)
-            for i in range(2):
-                got(lsef_out.at[i], l_recv.at[1 + i])
+
+
+def valid_row(x, c):
+    return ((x < 64) & (c % 2 == 1)) | ((x >= 64) & (x < 96) & (c % 4 >= 2)) | ((x >= 96) & (x < FAR) & (c >= 2))
 
 
 def picked(off_ref, level, bits):
@@ -636,43 +679,15 @@
 GROUP = 8
 
 
-def join_kernel(loc_ref, far_ref, lse_ref, lsef_ref, lsef2_ref, off_ref, out_ref, al_far, a_loc):
+def join_kernel(loc_ref, far_ref, al_far, a_loc, off_ref, out_ref):
     c = lax.axis_index("ctx") // 2
     lane = iota((1, DIM), 1)
 
-    def valid(x):
-        return ((x < 64) & (c % 2 == 1)) | ((x >= 64) & (x < 96) & (c % 4 >= 2)) | ((x >= 96) & (x < FAR) & (c >= 2))
-
-    @pl.when(pl.program_id(0) == 0)
-    def _():
-        one, two = [
-            jnp.concatenate([ref[0, 0], ref[1, 0], ref[0, 1], ref[1, 1]], axis=0) for ref in (lsef_ref, lsef2_ref)
-        ]
-        far = jnp.where((lane >= 96) & (c == 5), two, one)
-        far = jnp.where(valid(lane), far, NEG)
-        far3 = split3(far)
-        tall = iota((DIM, CHUNK), 0) + DIM
-        parts, spread, chosen = [lse_ref[...]], [], []
-        for level, (first, count, bits) in enumerate(REGIONS):
-            if level > 0:
-                hit = ((iota((DIM, CHUNK), 1) >> bits) == tall - first) & (tall >= first) & (tall < first + count)
-                spread.append(jnp.where(hit, 1.0, 0.0).astype(BF16))
-                chosen.append(picked(off_ref, level, bits))
-                parts.append(jnp.where(chosen[-1], fold3(nn(far3, spread[-1])), NEG))
-        lse = log_sum(parts)
-        back = jnp.zeros((2 * HEADS, DIM), F32)
-        for pick, wide in zip(chosen, spread):
-            back = back + fold3(nt(split3(jnp.where(pick, lse, 0.0)), wide))
-        al_far[...] = jnp.exp2(far - back)
-        share = jnp.exp2(lse_ref[...] - lse)
-        for b in range(2):
-            a_loc[b * CHUNK : (b + 1) * CHUNK] = upright(share, b)
-
+    sent = valid_row(iota((DIM, DIM), 0), c)
     row = lane + DIM
     first = jnp.where(row < 192, 128, jnp.where(row < 224, 192, 224))
     bits = jnp.where(row < 192, 2, jnp.where(row < 224, 3, 4))
     base = iota((CHUNK, DIM), 0) - ((row - first) << bits)
-    sent = valid(iota((DIM, DIM), 0))
     for i in range(GROUP):
         h = pl.program_id(0) * GROUP + i
         o2, o3, o4 = [off_ref[level, h] & (2 << level) - 1 for level in (1, 2, 3)]
@@ -693,17 +708,16 @@
     def vmem(*shape, kind=BF16):
         return pltpu.VMEM(shape, kind)
 
-    local, far, lse, lse_far, lse_far2 = pl.pallas_call(
+    local, far, far_share, local_share = pl.pallas_call(
         kernel,
         out_shape=(
             jax.ShapeDtypeStruct((HEADS, ROWS, DIM), BF16),
             jax.ShapeDtypeStruct((HEADS, 2, DIM, DIM), BF16),
-            jax.ShapeDtypeStruct((2 * HEADS, CHUNK), F32),
-            jax.ShapeDtypeStruct((2, 2, HALF, DIM), F32),
-            jax.ShapeDtypeStruct((2, 2, HALF, DIM), F32),
+            jax.ShapeDtypeStruct((2 * HEADS, DIM), F32),
+            jax.ShapeDtypeStruct((ROWS, DIM), F32),
         ),
         in_specs=[any_space] * 5,
-        out_specs=(any_space,) * 5,
+        out_specs=(any_space,) * 4,
         scratch_shapes=[
             vmem(1, ROWS, kind=I32), pltpu.SMEM((4, HEADS), I32), vmem(3, ROWS, HEADS * DIM),
             vmem(HALF, 3, 4, SEL, DIM), vmem(HALF, 3, 2, SEL, DIM), vmem(HALF, 4, FAR, DIM), vmem(HALF, 4, 16, DIM),
@@ -714,12 +728,13 @@
             vmem(2, 2, CHUNK, DIM, kind=F32), vmem(2, 2, DIM, DIM, kind=F32), vmem(2, 2, DIM, DIM, kind=F32),
             vmem(ROWS, DIM, kind=F32),
             vmem(2, 2, HALF, CHUNK, kind=F32), vmem(2, 2, HALF, DIM, kind=F32), vmem(2, 2, HALF, DIM, kind=F32),
-            vmem(2, HALF, CHUNK, kind=F32),
+            vmem(2, HALF, CHUNK, kind=F32), vmem(2, 2, HALF, DIM, kind=F32), vmem(2, 2, HALF, DIM, kind=F32),
             vmem(2 * HEADS, CHUNK, kind=F32),
             vmem(8, 1, ROWS, kind=I32), vmem(2 * DIM, CHUNK), vmem(4, 2 * DIM, CHUNK),
             vmem(SEL, CHUNK, kind=I32), vmem(CHUNK, CHUNK, kind=F32), vmem(2, CHUNK, CHUNK, kind=F32),
             vmem(2 * HEADS, CHUNK, kind=F32), vmem(ROWS, DIM, kind=F32),
-            dma((6,)), dma((17,)), dma((8,)), dma((HALF,)), dma((HALF,)), dma((HALF,)), dma((5,)),
+            vmem(2 * HEADS, DIM, kind=F32), vmem(ROWS, DIM, kind=F32),
+            dma((6,)), dma((18,)), dma((8,)), dma((HALF,)), dma((HALF,)), dma((HALF,)), dma((5,)),
         ],
         compiler_params=pltpu.CompilerParams(collective_id=0, has_side_effects=True, vmem_limit_bytes=56 << 20),
         name="dilated_attention",
@@ -733,14 +748,12 @@
             pl.BlockSpec((GROUP, 2, DIM, DIM), lambda i: (i, 0, 0, 0)),
             pl.BlockSpec(memory_space=pltpu.VMEM),
             pl.BlockSpec(memory_space=pltpu.VMEM),
-            pl.BlockSpec(memory_space=pltpu.VMEM),
             smem,
         ],
         out_specs=pl.BlockSpec((1, ROWS, GROUP * DIM), lambda i: (0, 0, i)),
-        scratch_shapes=[vmem(2 * HEADS, DIM, kind=F32), vmem(ROWS, DIM, kind=F32)],
         compiler_params=pltpu.CompilerParams(vmem_limit_bytes=60 << 20),
         name="join_far",
-    )(local, far, lse, lse_far, lse_far2, dilation_offsets)
+    )(local, far, far_share, local_share, dilation_offsets)
 
 
 def solution(mesh):

time: 38.7 us -> 37.9 us (0.979)
  Pallas kernels: 38.5 us -> 37.8 us
where the time goes in v3:
time: 37.9 us; the launch traced here: 37.8 us
  Pallas kernels  37.8 us (100%)
    pallas_call x1, Pallas kernels, on_device(): pl.pallas_call(kernel, out_shape=(jax.ShapeDtypeStruct((HEADS, ROWS, DIM)...  33.9 us
    pallas_call x1, Pallas kernels, on_device(): pl.pallas_call(join_kernel, grid=(HEADS // GROUP,), out_shape=jax.ShapeDt...  3.87 us

profile of v3, /device:TPU:111, one launch (start us, length us, event | category | flops | bytes accessed | tf_op | source)
XLA Modules:
  0.0 37.8 jit_solution(5506517175919084947)
XLA Ops:
  0.0 33.9 %dilated_attention.1 = (bf16[16,512,128]{2,1,0:T(8,128)(2,1)}, bf16[16,2,128,128]{3,2,1,0:T(8,128)(2,1)}, f32[32,128]{1,0:T(8,128)}, f32[512,128]{1,0:T(8,128)}) custom-call(bf16[1,512,2048]{2,1,0:T(8,128)(2,1)} %q_hbm.1, bf16[1,512,2048]{2,1,0:T(8,128)(2,1)} %k_hbm.1, bf16[1,512,2048]{2,1,0:T(8,128)(2,1)} %v_hbm.1, s32[1,512]{1,0:T(1,128)} %docs_hbm.1, ...), custom_call_target="tpu_custom_call" | custom-call | tf_op jit(solution)/shard_map/dilated_attention/pallas_call | solution.py:711
  34.0 3.9 %join_far.1 = bf16[1,512,2048]{2,1,0:T(8,128)(2,1)} custom-call(bf16[16,512,128]{2,1,0:T(8,128)(2,1)} %get-tuple-element.9.loc_ref, bf16[16,2,128,128]{3,2,1,0:T(8,128)(2,1)} %get-tuple-element.10.far_ref, f32[32,128]{1,0:T(8,128)} %get-tuple-element.11.al_far, f32[512,128]{1,0:T(8,128)} %get-tuple-element.12.a_loc, s32[4,16]{1,0:T(4,128)} %off_ref.1), custom_call_target="tpu_custom_call" | custom-call | tf_op jit(solution)/shard_map/join_far/pallas_call | solution.py:742

commit v4 on v3

--- a/solution.py
+++ b/solution.py
@@ -591,8 +591,11 @@
         back = back + fold3(nt(split3(jnp.where(pick, lse, 0.0)), wide))
     al_far[...] = jnp.exp2(far - back)
     portion = jnp.exp2(lse_loc[...] - lse)
-    for b in range(2):
-        share[b * CHUNK : (b + 1) * CHUNK] = upright(portion, b)
+    pad = jnp.zeros((DIM - GROUP, CHUNK), F32)
+    for g in range(HEADS // GROUP):
+        for b in range(2):
+            first = b * HEADS + g * GROUP
+            share[g, b * CHUNK : (b + 1) * CHUNK] = jnp.concatenate([portion[first : first + GROUP], pad], axis=0).T
     al_copy = pltpu.make_async_copy(al_far, al_out, al_sem)
     share_copy = pltpu.make_async_copy(share, share_out, lse_sem)
     al_copy.start()
@@ -696,7 +699,7 @@
             span = slice(b * CHUNK, (b + 1) * CHUNK)
             weight = jnp.where(hit, al_far[pl.ds(b * HEADS + h, 1), :], 0.0).astype(BF16)
             mixed = nn(weight, jnp.where(sent, far_ref[i, b], jnp.zeros((DIM, DIM), BF16)))
-            scale = jnp.sum(jnp.where(lane == h, a_loc[span], 0.0), axis=1, keepdims=True)
+            scale = a_loc[0, span, i : i + 1]
             out_ref[0, span, i * DIM : (i + 1) * DIM] = (mixed + scale * loc_ref[i, span].astype(F32)).astype(BF16)
 
 
@@ -714,7 +717,7 @@
             jax.ShapeDtypeStruct((HEADS, ROWS, DIM), BF16),
             jax.ShapeDtypeStruct((HEADS, 2, DIM, DIM), BF16),
             jax.ShapeDtypeStruct((2 * HEADS, DIM), F32),
-            jax.ShapeDtypeStruct((ROWS, DIM), F32),
+            jax.ShapeDtypeStruct((HEADS // GROUP, ROWS, DIM), F32),
         ),
         in_specs=[any_space] * 5,
         out_specs=(any_space,) * 4,
@@ -733,7 +736,7 @@
             vmem(8, 1, ROWS, kind=I32), vmem(2 * DIM, CHUNK), vmem(4, 2 * DIM, CHUNK),
             vmem(SEL, CHUNK, kind=I32), vmem(CHUNK, CHUNK, kind=F32), vmem(2, CHUNK, CHUNK, kind=F32),
             vmem(2 * HEADS, CHUNK, kind=F32), vmem(ROWS, DIM, kind=F32),
-            vmem(2 * HEADS, DIM, kind=F32), vmem(ROWS, DIM, kind=F32),
+            vmem(2 * HEADS, DIM, kind=F32), vmem(HEADS // GROUP, ROWS, DIM, kind=F32),
             dma((6,)), dma((18,)), dma((8,)), dma((HALF,)), dma((HALF,)), dma((HALF,)), dma((5,)),
         ],
         compiler_params=pltpu.CompilerParams(collective_id=0, has_side_effects=True, vmem_limit_bytes=56 << 20),
@@ -747,7 +750,7 @@
             pl.BlockSpec((GROUP, ROWS, DIM), lambda i: (i, 0, 0)),
             pl.BlockSpec((GROUP, 2, DIM, DIM), lambda i: (i, 0, 0, 0)),
             pl.BlockSpec(memory_space=pltpu.VMEM),
-            pl.BlockSpec(memory_space=pltpu.VMEM),
+            pl.BlockSpec((1, ROWS, DIM), lambda i: (i, 0, 0)),
             smem,
         ],
         out_specs=pl.BlockSpec((1, ROWS, GROUP * DIM), lambda i: (0, 0, i)),

time: 37.9 us -> 38.2 us (level)
  no operation moved by 1% of the time
where the time goes in v4:
time: 38.2 us; the launch traced here: 38.1 us
  Pallas kernels  38.1 us (100%)
    pallas_call x1, Pallas kernels, on_device(): pl.pallas_call(kernel, out_shape=(jax.ShapeDtypeStruct((HEADS, ROWS, DIM)...  33.9 us
    pallas_call x1, Pallas kernels, on_device(): pl.pallas_call(join_kernel, grid=(HEADS // GROUP,), out_shape=jax.ShapeDt...  4.16 us

profile of v4, /device:TPU:111, one launch (start us, length us, event | category | flops | bytes accessed | tf_op | source)
XLA Modules:
  0.0 38.1 jit_solution(4641453273672077720)
XLA Ops:
  0.0 33.9 %dilated_attention.1 = (bf16[16,512,128]{2,1,0:T(8,128)(2,1)}, bf16[16,2,128,128]{3,2,1,0:T(8,128)(2,1)}, f32[32,128]{1,0:T(8,128)}, f32[2,512,128]{2,1,0:T(8,128)}) custom-call(bf16[1,512,2048]{2,1,0:T(8,128)(2,1)} %q_hbm.1, bf16[1,512,2048]{2,1,0:T(8,128)(2,1)} %k_hbm.1, bf16[1,512,2048]{2,1,0:T(8,128)(2,1)} %v_hbm.1, s32[1,512]{1,0:T(1,128)} %docs_hbm.1, ...), custom_call_target="tpu_custom_call" | custom-call | tf_op jit(solution)/shard_map/dilated_attention/pallas_call | solution.py:714
  34.0 4.2 %join_far.1 = bf16[1,512,2048]{2,1,0:T(8,128)(2,1)} custom-call(bf16[16,512,128]{2,1,0:T(8,128)(2,1)} %get-tuple-element.9.loc_ref, bf16[16,2,128,128]{3,2,1,0:T(8,128)(2,1)} %get-tuple-element.10.far_ref, f32[32,128]{1,0:T(8,128)} %get-tuple-element.11.al_far, f32[2,512,128]{2,1,0:T(8,128)} %get-tuple-element.12.a_loc, s32[4,16]{1,0:T(4,128)} %off_ref.1), custom_call_target="tpu_custom_call" | custom-call | tf_op jit(solution)/shard_map/join_far/pallas_call | solution.py:745

commit v5 on v3

--- a/solution.py
+++ b/solution.py
@@ -121,8 +121,7 @@
     off_load = pltpu.make_async_copy(off_hbm, off_ref, load_sem.at[5])
     docs_load.start()
     off_load.start()
-    for u in range(4):
-        load_start(u)
+    load_start(0)
 
     for first, count, bits in REGIONS:
         base_m[first : first + count] = iota((count, CHUNK), 1) - (iota((count, CHUNK), 0) << bits)
@@ -227,6 +226,10 @@
         @pl.when(t % 2 == 0)
         def _():
             load_wait(t // 2)
+
+            @pl.when(t < 6)
+            def _():
+                load_start(t // 2 + 1)
 
         for which in range(2):
             h = HALF * (1 - j) + t if which == 0 else HALF * j + t

time: 37.9 us -> 38 us (level)
  no operation moved by 1% of the time
where the time goes in v5:
time: 38 us; the launch traced here: 37.8 us
  Pallas kernels  37.8 us (99%)
    pallas_call x1, Pallas kernels, on_device(): pl.pallas_call(kernel, out_shape=(jax.ShapeDtypeStruct((HEADS, ROWS, DIM)...  34 us
    pallas_call x1, Pallas kernels, on_device(): pl.pallas_call(join_kernel, grid=(HEADS // GROUP,), out_shape=jax.ShapeDt...  3.87 us

profile of v5, /device:TPU:111, one launch (start us, length us, event | category | flops | bytes accessed | tf_op | source)
XLA Modules:
  0.0 37.8 jit_solution(8187923828126499792)
XLA Ops:
  0.0 34.0 %dilated_attention.1 = (bf16[16,512,128]{2,1,0:T(8,128)(2,1)}, bf16[16,2,128,128]{3,2,1,0:T(8,128)(2,1)}, f32[32,128]{1,0:T(8,128)}, f32[512,128]{1,0:T(8,128)}) custom-call(bf16[1,512,2048]{2,1,0:T(8,128)(2,1)} %q_hbm.1, bf16[1,512,2048]{2,1,0:T(8,128)(2,1)} %k_hbm.1, bf16[1,512,2048]{2,1,0:T(8,128)(2,1)} %v_hbm.1, s32[1,512]{1,0:T(1,128)} %docs_hbm.1, ...), custom_call_target="tpu_custom_call" | custom-call | tf_op jit(solution)/shard_map/dilated_attention/pallas_call | solution.py:714
  34.0 3.9 %join_far.1 = bf16[1,512,2048]{2,1,0:T(8,128)(2,1)} custom-call(bf16[16,512,128]{2,1,0:T(8,128)(2,1)} %get-tuple-element.9.loc_ref, bf16[16,2,128,128]{3,2,1,0:T(8,128)(2,1)} %get-tuple-element.10.far_ref, f32[32,128]{1,0:T(8,128)} %get-tuple-element.11.al_far, f32[512,128]{1,0:T(8,128)} %get-tuple-element.12.a_loc, s32[4,16]{1,0:T(4,128)} %off_ref.1), custom_call_target="tpu_custom_call" | custom-call | tf_op jit(solution)/shard_map/join_far/pallas_call | solution.py:745
